TPU v7x, 32 devices: a whole 2x2x4 slice. The times are simulated.
32 devices in a mesh: parts: 2 (over y), tile: 4 (over z), tm: 2 (over x), rep: 2 (over core).
Axes of the slice: x: 2, y: 2, z: 4, core: 2. Of those that a mesh axis runs over, the one named last changes fastest.
Arguments:
- probes: bfloat16 [128, 4, 8192], P(('parts', 'rep'), 'tm', 'tile'), parts along dimension 0, may hold values from -6 to 6
- footprints: bfloat16 [128, 128, 2048], P(('parts', 'tile', 'tm')), parts along dimension 0, may hold values from -0.25 to 0.25
- owner_tile: int32 [128, 1], P(('parts', 'tile', 'tm')), parts along dimension 0, may hold values from 0 to 3; in each aligned block of 8 rows (0 to 7, 8 to 15, ...) at most 2 rows name the same one
- sounding_index: int32 [128], P(('parts', 'tile', 'tm')), parts along dimension 0, may hold values from 0 to 1
- flux_step: int32 [128], P(('parts', 'tile', 'tm')), parts along dimension 0, may hold values from 0 to 1
- entry_count: int32 [16], P(('parts', 'tile', 'tm')), parts along dimension 0, may hold values from 1 to 8
- departure: float32 [16, 128], P(('parts', 'tile', 'tm')), parts along dimension 0, may hold values from -12 to 12
- live_count: int32 [16], P(('parts', 'tile', 'tm')), parts along dimension 0, may hold values from 32 to 128
- error_id: int32 [16], P(('parts', 'tile', 'tm')), parts along dimension 0, may hold values from 0 to 3
- precision_table: float32 [4, 128, 128], replicated, may hold values from -1 to 2, as said below
- temporal_factor: float32 [4, 4], replicated, may hold values from -3 to 3
- row_factor: float32 [16, 16], replicated, may hold values from -1.5 to 1.5
- column_factor: float32 [128, 128], replicated, may hold values from -0.5 to 0.5
Outputs:
- gradient: bfloat16 [128, 4, 8192], P(('parts', 'rep'), 'tm', 'tile'), parts along dimension 0
There are 2 independent parts, one for each index of `parts`. A program takes and returns all parts, laid end to end along the dimension named above; an argument that names none is the same for every part. Nothing has to cross between parts.
Inputs may be any that keep to these rules, and one draw needn't show every extreme that they name: `owner_tile`: in the slots of one flux-holding device at most 2 name the same owner tile, and some device's slots reach 2. `precision_table`: each block is symmetric.
All inputs are finite; a program needn't handle non-finite values.
Results may differ from a plain program's by a relative error of at most 0.0061.
Values may be sent and summed in bfloat16 or wider, within the bound.
No kernel may reach another device: no remote copies, remote signals or barrier semaphores. Data moves between devices by JAX's collectives and lax.ppermute only.
A program may use at most 64 MiB of HBM per device.

v0:
```python
import jax
import jax.numpy as jnp
from jax import lax
from jax.sharding import PartitionSpec as P

highest = lax.Precision.HIGHEST


def spatial_forward(field, row_factor, column_factor):
    probe_count, steps, cells = field.shape
    rows = row_factor.shape[0]
    patch = field.reshape(probe_count, steps, rows, cells // rows)
    patch = jnp.einsum("ij,ptjc->ptic", row_factor, patch, precision=highest)
    patch = jnp.einsum("ptic,kc->ptik", patch, column_factor, precision=highest)
    return patch.reshape(probe_count, steps, cells)


def spatial_adjoint(field, row_factor, column_factor):
    probe_count, steps, cells = field.shape
    rows = row_factor.shape[0]
    patch = field.reshape(probe_count, steps, rows, cells // rows)
    patch = jnp.einsum("ij,ptic->ptjc", row_factor, patch, precision=highest)
    patch = jnp.einsum("ptjc,ck->ptjk", patch, column_factor, precision=highest)
    return patch.reshape(probe_count, steps, cells)


def weigh(predictions, departure, live_count, error_id, precision_table):
    block_rows = departure.shape[1]
    mask = (jnp.arange(block_rows)[None, :] < live_count[:, None]).astype(jnp.float32)
    residual = (predictions - departure[:, None, :]) * mask[:, None, :]
    choose = (error_id[:, None] == jnp.arange(precision_table.shape[0])[None, :]).astype(
        jnp.float32
    )
    precision = jnp.einsum("bn,nij->bij", choose, precision_table, precision=highest)
    weighted = jnp.einsum("bps,bsk->bpk", residual, precision, precision=highest) * mask[:, None, :]
    return weighted.astype(jnp.bfloat16)


def per_device(
    probes,
    footprints,
    owner_tile,
    sounding_index,
    flux_step,
    entry_count,
    departure,
    live_count,
    error_id,
    precision_table,
    temporal_factor,
    row_factor,
    column_factor,
):
    probe_count, steps, cells = probes.shape
    slots = footprints.shape[0]
    block_rows = footprints.shape[1]
    group_index = lax.axis_index("tm")
    own_rows = lax.dynamic_slice_in_dim(temporal_factor, group_index * steps, steps, 0)
    own_cols = lax.dynamic_slice_in_dim(temporal_factor, group_index * steps, steps, 1)
    field_zeros = jnp.zeros((probe_count, steps, cells), jnp.float32)
    factor = own_rows
    mixed = jnp.einsum(
        "tk,pks->pts",
        factor,
        lax.all_gather(probes, "tm", axis=1, tiled=True).astype(jnp.float32),
        precision=highest,
    )
    fluxes = spatial_forward(mixed, row_factor, column_factor).astype(jnp.bfloat16)
    count = entry_count[0]

    def predict(slot, partials):
        block = lax.dynamic_index_in_dim(fluxes, flux_step[slot], 1, keepdims=False)
        footprint = lax.dynamic_index_in_dim(footprints, slot, 0, keepdims=False)
        part = lax.dot_general(
            block, footprint, (((1,), (1,)), ((), ())), preferred_element_type=jnp.float32
        )
        return lax.dynamic_update_index_in_dim(partials, part, slot, 0)

    partials = lax.fori_loop(
        0, count, predict, jnp.zeros((slots, probe_count, block_rows), jnp.float32)
    )
    destination = owner_tile[:, 0]
    tile_count = lax.axis_size("tile")
    own_blocks = departure.shape[0]
    tile_blocks = own_blocks * lax.axis_size("tm")
    total_blocks = tile_blocks * tile_count
    target = destination * tile_blocks + sounding_index
    placing = (target[None, :] == jnp.arange(total_blocks)[:, None]).astype(jnp.float32)
    predictions = lax.psum_scatter(
        jnp.einsum("ne,epq->npq", placing, partials, precision=highest),
        ("tile", "tm"),
        scatter_dimension=0,
        tiled=True,
    )
    weights = weigh(predictions, departure, live_count, error_id, precision_table)
    every_weight = lax.all_gather(weights, ("tile", "tm"), axis=0, tiled=True)
    slot_weights = jnp.einsum(
        "ne,npq->epq",
        placing.astype(jnp.bfloat16),
        every_weight,
        preferred_element_type=jnp.float32,
    ).astype(jnp.bfloat16)

    def accumulate(slot, total):
        footprint = lax.dynamic_index_in_dim(footprints, slot, 0, keepdims=False)
        weight = lax.dynamic_index_in_dim(slot_weights, slot, 0, keepdims=False)
        term = jnp.dot(weight, footprint, preferred_element_type=jnp.float32)
        step = flux_step[slot]
        current = lax.dynamic_index_in_dim(total, step, 1, keepdims=False)
        return lax.dynamic_update_index_in_dim(total, current + term, step, 1)

    adjoint = lax.fori_loop(0, count, accumulate, field_zeros)
    back = spatial_adjoint(adjoint, row_factor, column_factor).astype(jnp.bfloat16)
    factor = own_cols
    pulled = jnp.einsum(
        "kt,pks->pts",
        factor,
        lax.all_gather(back, "tm", axis=1, tiled=True).astype(jnp.float32),
        precision=highest,
    )
    return (probes.astype(jnp.float32) + pulled).astype(jnp.bfloat16)


def solution(mesh):
    placed = (
        P(("parts", "rep"), "tm", "tile"),
        P(("parts", "tile", "tm"), None, None),
        P(("parts", "tile", "tm"), None),
        P(("parts", "tile", "tm")),
        P(("parts", "tile", "tm")),
        P(("parts", "tile", "tm")),
        P(("parts", "tile", "tm"), None),
        P(("parts", "tile", "tm")),
        P(("parts", "tile", "tm")),
        P(),
        P(),
        P(),
        P(),
    )
    return jax.shard_map(
        per_device,
        mesh=mesh,
        in_specs=placed,
        out_specs=P(("parts", "rep"), "tm", "tile"),
        check_vma=False,
    )
```

profile of v0, /device:TPU:0, one launch (start us, length us, event | category | flops | bytes accessed | tf_op | source)
XLA Modules:
  0.0 207.8 jit_solution(10734875581153441785)
XLA Ops:
  6.6 1.1 copy.25
  7.6 9.9 %all_gather.9 = bf16[32,4,2048]{2,0,1:T(8,128)(2,1)S(1)} all-gather(bf16[32,2,2048]{2,0,1:T(8,128)(2,1)S(1)} %copy.25), channel_id=1, replica_groups=mesh['parts'=2,'tile'=4,'tm'=2,'rep'=2] {'tm'}, dimensions={1}, use_global_device_ids=true | all-gather | bytes 786432 | tf_op jit(solution)/shard_map/all_gather | solution.py:65
  17.5 1.7 convolution_bitcast_fusion
  19.7 1.3 convolution_bitcast_fusion.3
  21.0 0.6 convolution_convert_fusion.1
  21.8 37.4 %while.20 = (s32[]{:T(128)}, f32[8,32,128]{2,0,1:T(8,128)S(1)}, s32[]{:T(128)}, s32[8]{0:T(128)S(1)}, bf16[32,2,2048]{2,0,1:T(8,128)(2,1)S(1)}, /*index=5*/bf16[...) while((s32[]{:T(128)}, f32[8,32,128]{2,0,1:T(8,128)S(1)}, s32[]{:T(128)}, ...), condition=%wide.region_1.2_spmd, body=%wide.region_0.1_spmd.sunk | while | flops 16777224 | bytes 704713 | solution.py:79
  22.5 0.7 dynamic_slice.67
  25.0 1.3 fusion.61
  27.0 0.7 dynamic_slice.67
  29.6 1.3 fusion.61
  31.6 0.7 dynamic_slice.67
  34.2 1.3 fusion.61
  36.2 0.7 dynamic_slice.67
  38.8 1.3 fusion.61
  40.8 0.7 dynamic_slice.67
  43.4 1.3 fusion.61
  45.4 0.7 dynamic_slice.67
  47.9 1.3 fusion.61
  50.0 0.7 dynamic_slice.67
  52.5 1.3 fusion.61
  54.6 0.7 dynamic_slice.67
  57.1 1.3 fusion.61
  59.6 0.7 copy.30
  61.6 0.5 fusion.19
  62.1 60.1 %reduce-scatter.2.cloned.1.call-done = f32[1,32,128]{2,1,0:T(8,128)} async-done(((f32[8,32,128]{2,1,0:T(8,128)}), f32[1,32,128]{2,1,0:T(8,128)}) %reduce-scatter.2.cloned.1.call-update) | async-done | bytes 16400 | tf_op jit(solution)/shard_map/reduce_scatter | solution.py:89
  122.2 0.9 fusion.15
  123.1 30.5 %all-gather = bf16[256,128]{1,0:T(8,128)(2,1)S(1)} all-gather(bf16[32,128]{1,0:T(8,128)(2,1)S(1)} %fusion.15), channel_id=2, replica_groups=mesh['parts'=2,'tile'=4,'tm'=2,'rep'=2] {'tile','tm'}, dimensions={0}, use_global_device_ids=true | all-gather | bytes 73728 | tf_op jit(solution)/shard_map/all_gather | solution.py:96
  153.9 36.6 %while.21 = (s32[]{:T(128)}, f32[32,2,2048]{2,0,1:T(8,128)S(1)}, s32[]{:T(128)}, s32[8]{0:T(128)S(1)}, bf16[8,32,128]{2,1,0:T(8,128)(2,1)S(1)}, /*index=5*/bf16[...) while((s32[]{:T(128)}, f32[32,2,2048]{2,0,1:T(8,128)S(1)}, s32[]{:T(128)}, ...), condition=%wide.region_4.5_spmd, body=%wide.region_3.4_spmd.sunk | while | flops 16842760 | bytes 1582785 | solution.py:112
  154.6 0.6 dynamic_slice.71
  157.1 1.2 fusion.64
  159.1 0.6 dynamic_slice.71
  161.6 1.3 fusion.64
  163.6 0.6 dynamic_slice.71
  166.1 1.2 fusion.64
  168.0 0.6 dynamic_slice.71
  170.6 1.3 fusion.64
  172.5 0.6 dynamic_slice.71
  175.1 1.2 fusion.64
  177.0 0.6 dynamic_slice.71
  179.6 1.3 fusion.64
  181.5 0.6 dynamic_slice.71
  184.1 1.2 fusion.64
  186.0 0.6 dynamic_slice.71
  188.6 1.3 fusion.64
  190.6 0.6 convolution_bitcast_fusion.2
  191.3 0.6 convolution_convert_fusion
  192.0 7.0 %all_gather.11 = bf16[32,4,2048]{2,0,1:T(8,128)(2,1)S(1)} all-gather(bf16[32,2,2048]{2,0,1:T(8,128)(2,1)S(1)} %copy.35), channel_id=1, replica_groups=mesh['parts'=2,'tile'=4,'tm'=2,'rep'=2] {'tm'}, dimensions={1}, use_global_device_ids=true | all-gather | bytes 786432 | tf_op jit(solution)/shard_map/all_gather | solution.py:118
  199.0 1.9 fusion.14
  (49 shorter events, 2.4 us)
Async XLA Ops:
  6.5 55.0 %copy-start = (f32[4,128,128]{2,1,0:T(8,128)S(1)}, f32[4,128,128]{2,1,0:T(8,128)}, u32[]{:S(2)}) copy-start(f32[4,128,128]{2,1,0:T(8,128)} %param.26) | copy-start | bytes 786436
  6.5 14.5 %copy-start.2 = (f32[128,128]{1,0:T(8,128)S(1)}, f32[128,128]{1,0:T(8,128)}, u32[]{:S(2)}) copy-start(f32[128,128]{1,0:T(8,128)} %param.29) | copy-start | bytes 196612
  6.5 15.2 %copy-start.8 = (s32[8]{0:T(128)S(1)}, s32[8]{0:T(128)}, u32[]{:S(2)}) copy-start(s32[8]{0:T(128)} %param.21) | copy-start | bytes 100
  6.5 115.7 %reduce-scatter.2.cloned.1.call-start = ((), (), s32[]{:S(2)}) async-start(), calls=%async_computation.1 | async-start | bytes 147456 | tf_op jit(solution)/shard_map/reduce_scatter | solution.py:89
  19.2 40.0 %copy-start.6 = (s32[8]{0:T(128)S(1)}, s32[8]{0:T(128)}, u32[]{:S(2)}) copy-start(s32[8]{0:T(128)} %param.20) | copy-start | bytes 100
  19.3 40.0 %copy-start.7 = (s32[8,1]{0,1:T(1,128)S(1)}, s32[8,1]{0,1:T(1,128)}, u32[]{:S(2)}) copy-start(s32[8,1]{0,1:T(1,128)} %param.19) | copy-start | bytes 100
  19.7 102.5 %copy-start.5 = (f32[1,128]{1,0:T(1,128)S(1)}, f32[1,128]{1,0:T(1,128)}, u32[]{:S(2)}) copy-start(f32[1,128]{1,0:T(1,128)} %param.23) | copy-start | bytes 1540
  153.9 36.7 %copy-start.3 = (f32[16,16]{1,0:T(8,128)S(1)}, f32[16,16]{1,0:T(8,128)}, u32[]{:S(2)}) copy-start(f32[16,16]{1,0:T(8,128)} %param.28) | copy-start | bytes 3076
  190.5 8.5 %copy-start.1 = (bf16[32,2,2048]{2,1,0:T(2,128)(2,1)S(1)}, bf16[32,2,2048]{2,1,0:T(2,128)(2,1)}, u32[]{:S(2)}) copy-start(bf16[32,2,2048]{2,1,0:T(2,128)(2,1)} %param.17) | copy-start | bytes 786436
  190.5 8.5 %copy-start.4 = (f32[4,4]{1,0:T(4,128)S(1)}, f32[4,4]{1,0:T(4,128)}, u32[]{:S(2)}) copy-start(f32[4,4]{1,0:T(4,128)} %param.27) | copy-start | bytes 196
Sparse Core Ops, SparseCore 0:
  60.4 61.7 reduce-scatter.1
where the time goes:
time: 208 us
  waiting for transfers between devices  60.1 us (29%)
  blocking collectives  47.5 us (23%)
  loops' own time  42.7 us (21%)
  matrix products  29.1 us (14%)
  between operations  14.9 us (7%)
  local copies, waits for them, and re-layouts  13.5 us (6%)
    reduce_scatter x1, waiting for transfers between devices, per_device(): lax.psum_scatter(jnp.einsum('ne,epq->npq', placing, partials, precision=h...  60.1 us
    all_gather x1, blocking collectives, per_device(): every_weight = lax.all_gather(weights, ('tile', 'tm'), axis=0, tiled=True)  30.5 us
    another operation x1, loops' own time, per_device(): adjoint = lax.fori_loop(0, count, accumulate, field_zeros)  21.7 us
    another operation x1, loops' own time, per_device(): lax.fori_loop(0, count, predict, jnp.zeros((slots, probe_count, block_row...  21 us
    dot_general x8, matrix products, predict(): lax.dot_general(block, footprint, (((1,), (1,)), ((), ())), preferred_ele...  10.5 us
    dot_general x8, matrix products, accumulate(): term = jnp.dot(weight, footprint, preferred_element_type=jnp.float32)  10 us
    all_gather x1, blocking collectives, per_device(): lax.all_gather(probes, 'tm', axis=1, tiled=True).astype(jnp.float32)  9.91 us
    all_gather x1, blocking collectives, per_device(): lax.all_gather(back, 'tm', axis=1, tiled=True).astype(jnp.float32)  7.05 us
  transfers between devices with their start and end apart: 1, of which 1 were waited for; matrix products, arithmetic and copies ran while one was open for 0% of the time, Pallas kernels for 0%

commit v1 on v0

v1 whole, which is shorter than its diff:
```python
import functools

import jax
import jax.numpy as jnp
from jax import lax
from jax.experimental import pallas as pl
from jax.experimental.pallas import tpu as pltpu
from jax.sharding import PartitionSpec as P

F32 = jnp.float32
BF16 = jnp.bfloat16
LANES = 128
VMEM_LIMIT = 12 * 1024 * 1024

in_vmem = pl.BlockSpec(memory_space=pltpu.VMEM)
in_hbm = pl.BlockSpec(memory_space=pltpu.HBM)
in_smem = pl.BlockSpec(memory_space=pltpu.SMEM)


def halves(value):
    high = value.astype(BF16)
    low = (value - high.astype(F32)).astype(BF16)
    return high, low


def widen(value):
    high, low = halves(value)
    return jnp.concatenate(
        [
            jnp.concatenate([high, low], axis=1),
            jnp.concatenate([high, jnp.zeros_like(low)], axis=1),
        ],
        axis=0,
    )


def times_wide(value, wide):
    high, low = halves(value)
    both = jnp.dot(
        jnp.concatenate([high, low], axis=1), wide, preferred_element_type=F32
    )
    size = both.shape[1] // 2
    return both[:, :size] + both[:, size:]


def mixing(factor, group, groups, steps, count, forward):
    block = steps * count
    row = lax.broadcasted_iota(jnp.int32, (block, groups * block), 0)
    col = lax.broadcasted_iota(jnp.int32, (block, groups * block), 1)
    peer, within = lax.div(col, block), lax.rem(col, block)
    if forward:
        row_step, row_probe = lax.div(row, count), lax.rem(row, count)
        col_probe, col_step = lax.div(within, steps), lax.rem(within, steps)
    else:
        row_probe, row_step = lax.div(row, steps), lax.rem(row, steps)
        col_step, col_probe = lax.div(within, count), lax.rem(within, count)
    value = jnp.zeros((block, groups * block), F32)
    same = row_probe == col_probe
    for other in range(groups):
        for a in range(steps):
            for b in range(steps):
                mine, theirs = group * steps + a, (group ^ other) * steps + b
                scale = factor[mine, theirs] if forward else factor[theirs, mine]
                here = same & (peer == other) & (row_step == a) & (col_step == b)
                value = jnp.where(here, scale, value)
    return jnp.concatenate(halves(value), axis=0)


def prepare_kernel(
    groups, steps, count, blocks, own_blocks,
    footprints, table, temporal, row_factor, column, owner, sounding, flux_step,
    departure, entries, live_count, error_id,
    held, table_at, rows_at, mix_f, mix_b, wide_f, wide_b, base, place, step_of,
    factor, column_at, owner_at, sounding_at, flux_at, departure_at, sems,
):
    pairs = [
        (temporal, factor), (column, column_at), (departure, departure_at), (owner, owner_at),
        (sounding, sounding_at), (flux_step, flux_at), (row_factor, rows_at),
        (table, table_at), (footprints, held),
    ]
    copies = [pltpu.make_async_copy(a, b, sems.at[n]) for n, (a, b) in enumerate(pairs)]
    for copy in copies:
        copy.start()
    for copy in copies[:-2]:
        copy.wait()
    group = lax.axis_index("tm")
    mix_f[...] = mixing(factor, group, groups, steps, count, True)
    mix_b[...] = mixing(factor, group, groups, steps, count, False)
    wide_f[...] = widen(column_at[...].T)
    wide_b[...] = widen(column_at[...])
    base[...] = jnp.zeros_like(base)
    block_rows = base.shape[1]
    for q in range(own_blocks):
        at = (lax.axis_index("tile") * groups + group) * own_blocks + q
        base[pl.ds(pl.multiple_of(at * count, count), count), :] = jnp.broadcast_to(
            -departure_at[q : q + 1, :], (count, block_rows)
        )
        base[pl.ds(blocks * count + at, 1), :] = jnp.full(
            (1, block_rows), live_count[q].astype(F32)
        )
        base[pl.ds(blocks * count + blocks + at, 1), :] = jnp.full(
            (1, block_rows), error_id[q].astype(F32)
        )
    for e in range(place.shape[0]):
        place[e] = owner_at[e] * (groups * own_blocks) + sounding_at[e]
        step_of[e] = jnp.where(e < entries[0], flux_at[e], steps)
    for copy in copies[-2:]:
        copy.wait()


def row_mix(field, row_factor, transposed, wide, place):
    rows = row_factor.shape[0]
    batch = 4
    for start in range(0, rows, batch):
        sums = [None] * batch
        for j in range(rows):
            tile = field[:, j * LANES : (j + 1) * LANES]
            for n in range(batch):
                i = start + n
                scale = row_factor[j, i] if transposed else row_factor[i, j]
                term = scale * tile
                sums[n] = term if sums[n] is None else sums[n] + term
        result = times_wide(jnp.concatenate(sums, axis=0), wide).astype(BF16)
        size = sums[0].shape[0]
        for n in range(batch):
            i = start + n
            place[:, i * LANES : (i + 1) * LANES] = result[n * size : (n + 1) * size]


def predict_kernel(groups, steps, count, *refs):
    fields = refs[:groups]
    (
        mix_f, row_factor, wide_f, held, base, place, step_of, total,
        mixed, fluxes,
    ) = refs[groups:]
    slots = place.shape[0]
    block_rows = base.shape[1]
    stacked = jnp.concatenate(
        [fields[0][...]] + [f[...].reshape(fields[0].shape) for f in fields[1:]], axis=0
    )
    both = jnp.dot(mix_f[...], stacked, preferred_element_type=F32)
    size = steps * count
    mixed[...] = both[:size] + both[size:]
    row_mix(mixed, row_factor, False, wide_f[...], fluxes)
    total[...] = base[...]
    flux = fluxes[...]
    for e in range(slots):
        part = lax.dot_general(
            flux,
            held[e * block_rows : (e + 1) * block_rows, :],
            (((1,), (1,)), ((), ())),
            preferred_element_type=F32,
        )
        chosen = jnp.zeros((count, block_rows), F32)
        for t in range(steps):
            chosen = jnp.where(step_of[e] == t, part[t * count : (t + 1) * count], chosen)
        at = pl.ds(pl.multiple_of(place[e] * count, count), count)
        total[at, :] = total[at, :] + chosen


def adjoint_kernel(
    steps, count, blocks,
    total, table, row_factor, wide_b, held, place, step_of,
    back, weights, adjoint,
):
    block_rows = table.shape[1]
    slots = place.shape[0]
    lane = lax.broadcasted_iota(jnp.int32, (1, block_rows), 1).astype(F32)
    for e in range(slots):
        target = place[e]
        live = total[pl.ds(blocks * count + target, 1), :]
        error = total[pl.ds(blocks * count + blocks + target, 1), :]
        mask = jnp.where(lane < live, 1.0, 0.0)
        residual = total[pl.ds(pl.multiple_of(target * count, count), count), :] * mask
        precision = table[0]
        for n in range(1, table.shape[0]):
            precision = jnp.where(error == n, table[n], precision)
        weight = times_wide(residual, widen(precision)) * mask
        for t in range(steps):
            weights[t * count : (t + 1) * count, e * block_rows : (e + 1) * block_rows] = (
                jnp.where(step_of[e] == t, weight, 0.0).astype(BF16)
            )
    adjoint[...] = jnp.dot(weights[...], held[...], preferred_element_type=F32)
    row_mix(adjoint, row_factor, True, wide_b[...], back)


def finish_kernel(groups, *refs):
    backs = refs[:groups]
    probes, mix_b, out = refs[groups:]
    stacked = jnp.concatenate([b[...] for b in backs], axis=0)
    both = jnp.dot(mix_b[...], stacked, preferred_element_type=F32)
    size = out.shape[0]
    out[...] = (probes[...].astype(F32) + (both[:size] + both[size:])).astype(BF16)


def exchange(value, axis, distance):
    size = lax.axis_size(axis)
    return lax.ppermute(value, axis, [(i, i ^ distance) for i in range(size)])


def subsets(spans):
    choices = [[]]
    for span in spans:
        choices = choices + [c + [span] for c in choices]
    return choices[:0:-1]


def hop(value, moves):
    tiles, groups = lax.axis_size("tile"), lax.axis_size("tm")
    flip = sum(d * groups if axis == "tile" else d for axis, d in moves)
    return lax.ppermute(
        value, ("tile", "tm"), [(i, i ^ flip) for i in range(tiles * groups)]
    )


def everywhere(value):
    spans = [
        (axis, 1 << n)
        for axis in ("tm", "tile")
        for n in range(lax.axis_size(axis).bit_length() - 1)
    ]
    for start in range(0, len(spans), 2):
        sent = value.astype(BF16)
        terms = [hop(sent, moves) for moves in subsets(spans[start : start + 2])]
        for term in terms:
            value = value + term.astype(F32)
    return value


def outside(*values):
    return [pltpu.with_memory_space_constraint(x, pltpu.HBM) for x in values]


def per_device(
    probes,
    footprints,
    owner_tile,
    sounding_index,
    flux_step,
    entry_count,
    departure,
    live_count,
    error_id,
    precision_table,
    temporal_factor,
    row_factor,
    column_factor,
):
    count, steps, cells = probes.shape
    slots, block_rows = footprints.shape[:2]
    groups = lax.axis_size("tm")
    own_blocks = departure.shape[0]
    blocks = own_blocks * groups * lax.axis_size("tile")
    size = steps * count
    params = pltpu.CompilerParams(vmem_limit_bytes=VMEM_LIMIT)

    peers = [exchange(probes, "tm", d) for d in range(1, groups)]
    own = probes.reshape(size, cells)
    held, table, rows, mix_f, mix_b, wide_f, wide_b, base, place, step_of = pl.pallas_call(
        functools.partial(prepare_kernel, groups, steps, count, blocks, own_blocks),
        out_shape=[
            pltpu.VMEM((slots * block_rows, cells), BF16),
            pltpu.VMEM(precision_table.shape, F32),
            pltpu.SMEM(row_factor.shape, F32),
            pltpu.VMEM((2 * size, groups * size), BF16),
            pltpu.VMEM((2 * size, groups * size), BF16),
            pltpu.VMEM((2 * LANES, 2 * LANES), BF16),
            pltpu.VMEM((2 * LANES, 2 * LANES), BF16),
            pltpu.VMEM((blocks * (count + 2), block_rows), F32),
            pltpu.SMEM((slots,), jnp.int32),
            pltpu.SMEM((slots,), jnp.int32),
        ],
        in_specs=[in_hbm] * 9 + [in_smem] * 3,
        out_specs=[in_vmem] * 2 + [in_smem] + [in_vmem] * 5 + [in_smem] * 2,
        scratch_shapes=[
            pltpu.SMEM(temporal_factor.shape, F32),
            pltpu.VMEM(column_factor.shape, F32),
            pltpu.SMEM((slots,), jnp.int32),
            pltpu.SMEM((slots,), jnp.int32),
            pltpu.SMEM((slots,), jnp.int32),
            pltpu.VMEM(departure.shape, F32),
            pltpu.SemaphoreType.DMA((9,)),
        ],
        compiler_params=params,
        name="prepare",
    )(
        *outside(
            footprints.reshape(slots * block_rows, cells), precision_table, temporal_factor, row_factor, column_factor,
            owner_tile.reshape(slots), sounding_index, flux_step, departure,
        ),
        entry_count, live_count, error_id,
    )
    held, table, mix_f, mix_b, wide_f, wide_b, base = [
        pltpu.with_memory_space_constraint(x, pltpu.VMEM)
        for x in (held, table, mix_f, mix_b, wide_f, wide_b, base)
    ]

    total = pl.pallas_call(
        functools.partial(predict_kernel, groups, steps, count),
        out_shape=jax.ShapeDtypeStruct(base.shape, F32),
        in_specs=[in_vmem] * (groups + 1) + [in_smem] + [in_vmem] * 3 + [in_smem] * 2,
        out_specs=in_vmem,
        scratch_shapes=[
            pltpu.VMEM((size, cells), F32),
            pltpu.VMEM((size, cells), BF16),
        ],
        compiler_params=params,
        name="predict",
    )(
        own, *peers,
        mix_f, rows, wide_f, held, base, place, step_of,
    )
    total = everywhere(total)

    back = pl.pallas_call(
        functools.partial(adjoint_kernel, steps, count, blocks),
        out_shape=jax.ShapeDtypeStruct((size, cells), BF16),
        in_specs=[in_vmem] * 2 + [in_smem] + [in_vmem] * 2 + [in_smem] * 2,
        out_specs=in_vmem,
        scratch_shapes=[
            pltpu.VMEM((size, slots * block_rows), BF16),
            pltpu.VMEM((size, cells), F32),
        ],
        compiler_params=params,
        name="adjoint",
    )(total, table, rows, wide_b, held, place, step_of)

    backs = [back] + [exchange(back, "tm", d) for d in range(1, groups)]
    result = pl.pallas_call(
        functools.partial(finish_kernel, groups),
        out_shape=jax.ShapeDtypeStruct((size, cells), BF16),
        in_specs=[in_vmem] * (groups + 2),
        out_specs=in_vmem,
        compiler_params=params,
        name="finish",
    )(*backs, own, mix_b)
    return result.reshape(count, steps, cells)


def solution(mesh):
    placed = (
        P(("parts", "rep"), "tm", "tile"),
        P(("parts", "tile", "tm"), None, None),
        P(("parts", "tile", "tm"), None),
        P(("parts", "tile", "tm")),
        P(("parts", "tile", "tm")),
        P(("parts", "tile", "tm")),
        P(("parts", "tile", "tm"), None),
        P(("parts", "tile", "tm")),
        P(("parts", "tile", "tm")),
        P(),
        P(),
        P(),
        P(),
    )
    return jax.shard_map(
        per_device,
        mesh=mesh,
        in_specs=placed,
        out_specs=P(("parts", "rep"), "tm", "tile"),
        check_vma=False,
    )
```

time: 208 us -> 35.6 us (0.17)
  blocking collectives: 47.5 us -> 0 us
  waiting for transfers between devices: 60.1 us -> 14.4 us
  loops' own time: 42.7 us -> 0 us
  matrix products: 29.1 us -> 0 us
  between operations: 14.9 us -> 1.99 us
  local copies, waits for them, and re-layouts: 13.5 us -> 1.97 us
  starting transfers between devices: 0.01 us -> 10.5 us
  Pallas kernels: 0 us -> 6.47 us
    reduce_scatter x1 -> x0, waiting for transfers between devices: 60.1 us -> none  [per_device(): lax.psum_scatter(jnp.einsum('ne,epq->npq', placing, partials, precision=h...]
    all_gather x3 -> x0, blocking collectives: 47.5 us -> none  [the longest x1 30.5 us: per_device(): every_weight = lax.all_gather(weights, ('tile', 'tm'), axis=0, tiled=True)]
    another operation x2 -> x0, loops' own time: 42.7 us -> none  [the longest x1 21.7 us: per_device(): adjoint = lax.fori_loop(0, count, accumulate, field_zeros)]
    dot_general x26 -> x0, matrix products: 29.1 us -> none  [the longest x8 10.5 us: predict(): lax.dot_general(block, footprint, (((1,), (1,)), ((), ())), preferred_ele...]
    ppermute x0 -> x6, waiting for transfers between devices: none -> 14.4 us  [the longest x4 7.65 us: hop(): lax.ppermute(value, ('tile', 'tm'), [(i, i ^ flip) for i in range(tiles *...]
    ppermute x0 -> x6, starting transfers between devices: none -> 10.5 us  [the longest x4 6.84 us: hop(): lax.ppermute(value, ('tile', 'tm'), [(i, i ^ flip) for i in range(tiles *...]
    dynamic_slice x24 -> x0, local copies, waits for them, and re-layouts: 10.1 us -> none  [the longest x8 5.2 us: predict(): block = lax.dynamic_index_in_dim(fluxes, flux_step[slot], 1, keepdims=False)]
    pallas_call x0 -> x4, Pallas kernels: none -> 6.47 us  [the longest x1 2.42 us: per_device(): pl.pallas_call(functools.partial(prepare_kernel, groups, steps, count, bl...]
  transfers between devices with their start and end apart: 1 -> 6, of which waited for: 1 -> 6; matrix products, arithmetic and copies ran while one was open for 0% -> 3% of each run, Pallas kernels for 0% -> 7%
where the time goes in v1:
time: 35.6 us; the launch traced here: 35.4 us
  waiting for transfers between devices  14.4 us (40%)
  starting transfers between devices  10.5 us (29%)
  Pallas kernels  6.47 us (18%)
  between operations  1.99 us (6%)
  local copies, waits for them, and re-layouts  1.97 us (6%)
    ppermute x4, waiting for transfers between devices, hop(): lax.ppermute(value, ('tile', 'tm'), [(i, i ^ flip) for i in range(tiles *...  7.65 us
    ppermute x4, starting transfers between devices, hop(): lax.ppermute(value, ('tile', 'tm'), [(i, i ^ flip) for i in range(tiles *...  6.84 us
    ppermute x2, waiting for transfers between devices, exchange(): return lax.ppermute(value, axis, [(i, i ^ distance) for i in range(size)])  6.78 us
    ppermute x2, starting transfers between devices, exchange(): return lax.ppermute(value, axis, [(i, i ^ distance) for i in range(size)])  3.66 us
    pallas_call x1, Pallas kernels, per_device(): pl.pallas_call(functools.partial(prepare_kernel, groups, steps, count, bl...  2.42 us
    pallas_call x1, Pallas kernels, per_device(): pl.pallas_call(functools.partial(predict_kernel, groups, steps, count), o...  2.26 us
    pallas_call x1, Pallas kernels, per_device(): pl.pallas_call(functools.partial(adjoint_kernel, steps, count, blocks), o...  1.51 us
    reshape x1, local copies, waits for them, and re-layouts, per_device(): own = probes.reshape(size, cells)  1.08 us
  transfers between devices with their start and end apart: 6, of which 6 were waited for; matrix products, arithmetic and copies ran while one was open for 3% of the time, Pallas kernels for 7%

profile of v1, /device:TPU:0, one launch (start us, length us, event | category | flops | bytes accessed | tf_op | source)
XLA Modules:
  0.0 35.4 jit_solution(18337972810385817926)
XLA Ops:
  0.0 2.9 %collective-permute-start = (bf16[32,2,2048]{2,1,0:T(2,128)(2,1)}, bf16[32,2,2048]{2,1,0:T(2,128)(2,1)S(1)}, u32[]{:S(2)}, u32[]{:S(2)}) collective-permute-start(bf16[32,2,2048]{2,1,0:T(2,128)(2,1)} %param.13), channel_id=1, source_target_pairs={{0,2},{2,0},{1,3},{3,1},{4,6},{6,4},{5,7},{7,5},{8,10},{10,8},{9,1... | collective-permute-start | bytes 786440 | tf_op jit(solution)/shard_map/ppermute | solution.py:198
  2.9 1.1 %reshape.12.refs_0_.refs_2_ = bf16[64,2048]{1,0:T(8,128)(2,1)S(1)} reshape(bf16[32,2,2048]{2,1,0:T(2,128)(2,1)} %param.13) | data formatting | bytes 524288 | tf_op jit(solution)/shard_map/reshape | solution.py:258
  6.0 2.4 %prepare.1 = (bf16[1024,2048]{1,0:T(8,128)(2,1)S(1)}, f32[4,128,128]{2,1,0:T(8,128)S(1)}, f32[16,16]{1,0:T(8,128)S(4)}, bf16[128,128]{1,0:T(8,128)(2,1)S(1)}, bf...) custom-call(bf16[1024,2048]{1,0:T(8,128)(2,1)} %bitcast.2, ...), custom_call_target="tpu_custom_call" | custom-call | tf_op jit(solution)/shard_map/prepare/pallas_call | solution.py:259
  8.4 1.1 %collective-permute-done.refs_1_ = bf16[32,2,2048]{2,1,0:T(2,128)(2,1)S(1)} collective-permute-done((bf16[32,2,2048]{2,1,0:T(2,128)(2,1)}, bf16[32,2,2048]{2,1,0:T(2,128)(2,1)S(1)}, u32[]{:S(2)}, u32[]{:S(2)}) %collective-permute-start) | collective-permute-done | bytes 262176 | tf_op jit(solution)/shard_map/ppermute | solution.py:198
  9.5 2.3 %predict.1 = f32[272,128]{1,0:T(8,128)S(1)} custom-call(bf16[64,2048]{1,0:T(8,128)(2,1)S(1)} %reshape.12.refs_0_.refs_2_, bf16[32,2,2048]{2,1,0:T(2,128)(2,1)S(1)} %collective-permute-done.refs_1_, bf16[128,128]{1,0:T(8,128)(2,1)S(1)} %get-tuple-element.15.refs_2_, f32[16,16]{1,0:T(8,128)S(4)} %get-tuple-element.16.refs_3_.row_factor, ...), custom_call_target="tpu_custom_call" | custom-call | tf_op jit(solution)/shard_map/predict/pallas_call | solution.py:298
  11.7 1.8 %collective-permute-start.3 = (bf16[272,128]{1,0:T(8,128)(2,1)S(1)}, bf16[272,128]{1,0:T(8,128)(2,1)S(1)}, u32[]{:S(2)}, u32[]{:S(2)}) collective-permute-start(bf16[272,128]{1,0:T(8,128)(2,1)S(1)} %convert_element_type.18), channel_id=1, source_target_pairs={{0,2},{2,0},{4,6},{6,4},{8,10},{10,8},{12,14},{14,12},{1,3},{3,1},... | collective-permute-start | bytes 208904 | tf_op jit(solution)/shard_map/ppermute | solution.py:211
  13.5 1.6 %collective-permute-start.2 = (bf16[272,128]{1,0:T(8,128)(2,1)S(1)}, bf16[272,128]{1,0:T(8,128)(2,1)S(1)}, u32[]{:S(2)}, u32[]{:S(2)}) collective-permute-start(bf16[272,128]{1,0:T(8,128)(2,1)S(1)} %convert_element_type.18), channel_id=1, source_target_pairs={{0,4},{2,6},{4,0},{6,2},{8,12},{10,14},{12,8},{14,10},{1,5},{3,7},... | collective-permute-start | bytes 208904 | tf_op jit(solution)/shard_map/ppermute | solution.py:211
  15.1 0.2 collective-permute-start.1
  15.3 0.9 %collective-permute-done.3 = bf16[272,128]{1,0:T(8,128)(2,1)S(1)} collective-permute-done((bf16[272,128]{1,0:T(8,128)(2,1)S(1)}, bf16[272,128]{1,0:T(8,128)(2,1)S(1)}, u32[]{:S(2)}, u32[]{:S(2)}) %collective-permute-start.3) | collective-permute-done | bytes 69664 | tf_op jit(solution)/shard_map/ppermute | solution.py:211
  16.2 1.7 %collective-permute-done.2 = bf16[272,128]{1,0:T(8,128)(2,1)S(1)} collective-permute-done((bf16[272,128]{1,0:T(8,128)(2,1)S(1)}, bf16[272,128]{1,0:T(8,128)(2,1)S(1)}, u32[]{:S(2)}, u32[]{:S(2)}) %collective-permute-start.2) | collective-permute-done | bytes 69664 | tf_op jit(solution)/shard_map/ppermute | solution.py:211
  17.9 2.5 %collective-permute-done.1 = bf16[272,128]{1,0:T(8,128)(2,1)S(1)} collective-permute-done((bf16[272,128]{1,0:T(8,128)(2,1)S(1)}, bf16[272,128]{1,0:T(8,128)(2,1)S(1)}, u32[]{:S(2)}, u32[]{:S(2)}) %collective-permute-start.1) | collective-permute-done | bytes 69664 | tf_op jit(solution)/shard_map/ppermute | solution.py:211
  20.4 3.3 %collective-permute-start.4 = (bf16[272,128]{1,0:T(8,128)(2,1)S(1)}, bf16[272,128]{1,0:T(8,128)(2,1)S(1)}, u32[]{:S(2)}, u32[]{:S(2)}) collective-permute-start(bf16[272,128]{1,0:T(8,128)(2,1)S(1)} %fusion), channel_id=1, source_target_pairs={{0,8},{2,10},{4,12},{6,14},{8,0},{10,2},{12,4},{14,6},{1,9},{3,11}... | collective-permute-start | bytes 208904 | tf_op jit(solution)/shard_map/ppermute | solution.py:211
  23.7 2.6 %collective-permute-done.4 = bf16[272,128]{1,0:T(8,128)(2,1)S(1)} collective-permute-done((bf16[272,128]{1,0:T(8,128)(2,1)S(1)}, bf16[272,128]{1,0:T(8,128)(2,1)S(1)}, u32[]{:S(2)}, u32[]{:S(2)}) %collective-permute-start.4) | collective-permute-done | bytes 69664 | tf_op jit(solution)/shard_map/ppermute | solution.py:211
  26.3 1.5 %adjoint.1.refs_0_ = bf16[64,2048]{1,0:T(8,128)(2,1)S(1)} custom-call(f32[272,128]{1,0:T(8,128)S(1)} %convert_add_fusion.total, f32[4,128,128]{2,1,0:T(8,128)S(1)} %get-tuple-element.22.table, f32[16,16]{1,0:T(8,128)S(4)} %get-tuple-element.16.refs_3_.row_factor, bf16[256,256]{1,0:T(8,128)(2,1)S(1)} %get-tuple-element.23.wide_b, ...), custom_call_target="tpu_custom_call" | custom-call | tf_op jit(solution)/shard_map/adjoint/pallas_call | solution.py:315
  27.8 0.7 %collective-permute-start.5 = (bf16[64,2048]{1,0:T(8,128)(2,1)S(1)}, bf16[64,2048]{1,0:T(8,128)(2,1)S(1)}, u32[]{:S(2)}, u32[]{:S(2)}) collective-permute-start(bf16[64,2048]{1,0:T(8,128)(2,1)S(1)} %adjoint.1.refs_0_), channel_id=1, source_target_pairs={{0,2},{2,0},{1,3},{3,1},{4,6},{6,4},{5,7},{7,5},{8,10},{10,8},{9,1... | collective-permute-start | bytes 786440 | tf_op jit(solution)/shard_map/ppermute | solution.py:198
  28.6 5.7 %collective-permute-done.5.refs_1_ = bf16[64,2048]{1,0:T(8,128)(2,1)S(1)} collective-permute-done((bf16[64,2048]{1,0:T(8,128)(2,1)S(1)}, bf16[64,2048]{1,0:T(8,128)(2,1)S(1)}, u32[]{:S(2)}, u32[]{:S(2)}) %collective-permute-start.5) | collective-permute-done | bytes 262176 | tf_op jit(solution)/shard_map/ppermute | solution.py:198
  34.3 0.3 finish.1
  34.6 0.9 %reshape.15 = bf16[32,2,2048]{2,1,0:T(2,128)(2,1)} reshape(bf16[64,2048]{1,0:T(8,128)(2,1)S(1)} %finish.1) | data formatting | bytes 524288 | tf_op jit(solution)/shard_map/reshape | solution.py:337
  (3 shorter events, 0.1 us)
Async XLA Ops:
  0.0 9.5 %collective-permute-start = (bf16[32,2,2048]{2,1,0:T(2,128)(2,1)}, bf16[32,2,2048]{2,1,0:T(2,128)(2,1)S(1)}, u32[]{:S(2)}, u32[]{:S(2)}) collective-permute-start(bf16[32,2,2048]{2,1,0:T(2,128)(2,1)} %param.13), channel_id=1, source_target_pairs={{0,2},{2,0},{1,3},{3,1},{4,6},{6,4},{5,7},{7,5},{8,10},{10,8},{9,1... | collective-permute-start | bytes 786440 | tf_op jit(solution)/shard_map/ppermute | solution.py:198
  11.7 4.4 %collective-permute-start.3 = (bf16[272,128]{1,0:T(8,128)(2,1)S(1)}, bf16[272,128]{1,0:T(8,128)(2,1)S(1)}, u32[]{:S(2)}, u32[]{:S(2)}) collective-permute-start(bf16[272,128]{1,0:T(8,128)(2,1)S(1)} %convert_element_type.18), channel_id=1, source_target_pairs={{0,2},{2,0},{4,6},{6,4},{8,10},{10,8},{12,14},{14,12},{1,3},{3,1},... | collective-permute-start | bytes 208904 | tf_op jit(solution)/shard_map/ppermute | solution.py:211
  13.5 4.3 %collective-permute-start.2 = (bf16[272,128]{1,0:T(8,128)(2,1)S(1)}, bf16[272,128]{1,0:T(8,128)(2,1)S(1)}, u32[]{:S(2)}, u32[]{:S(2)}) collective-permute-start(bf16[272,128]{1,0:T(8,128)(2,1)S(1)} %convert_element_type.18), channel_id=1, source_target_pairs={{0,4},{2,6},{4,0},{6,2},{8,12},{10,14},{12,8},{14,10},{1,5},{3,7},... | collective-permute-start | bytes 208904 | tf_op jit(solution)/shard_map/ppermute | solution.py:211
  15.1 5.2 %collective-permute-start.1 = (bf16[272,128]{1,0:T(8,128)(2,1)S(1)}, bf16[272,128]{1,0:T(8,128)(2,1)S(1)}, u32[]{:S(2)}, u32[]{:S(2)}) collective-permute-start(bf16[272,128]{1,0:T(8,128)(2,1)S(1)} %convert_element_type.18), channel_id=1, source_target_pairs={{0,6},{2,4},{4,2},{6,0},{8,14},{10,12},{12,10},{14,8},{1,7},{3,5},... | collective-permute-start | bytes 208904 | tf_op jit(solution)/shard_map/ppermute | solution.py:211
  20.4 5.9 %collective-permute-start.4 = (bf16[272,128]{1,0:T(8,128)(2,1)S(1)}, bf16[272,128]{1,0:T(8,128)(2,1)S(1)}, u32[]{:S(2)}, u32[]{:S(2)}) collective-permute-start(bf16[272,128]{1,0:T(8,128)(2,1)S(1)} %fusion), channel_id=1, source_target_pairs={{0,8},{2,10},{4,12},{6,14},{8,0},{10,2},{12,4},{14,6},{1,9},{3,11}... | collective-permute-start | bytes 208904 | tf_op jit(solution)/shard_map/ppermute | solution.py:211
  27.8 6.4 %collective-permute-start.5 = (bf16[64,2048]{1,0:T(8,128)(2,1)S(1)}, bf16[64,2048]{1,0:T(8,128)(2,1)S(1)}, u32[]{:S(2)}, u32[]{:S(2)}) collective-permute-start(bf16[64,2048]{1,0:T(8,128)(2,1)S(1)} %adjoint.1.refs_0_), channel_id=1, source_target_pairs={{0,2},{2,0},{1,3},{3,1},{4,6},{6,4},{5,7},{7,5},{8,10},{10,8},{9,1... | collective-permute-start | bytes 786440 | tf_op jit(solution)/shard_map/ppermute | solution.py:198

commit v2 on v1

--- a/solution.py
+++ b/solution.py
@@ -68,20 +68,29 @@
 
 def prepare_kernel(
     groups, steps, count, blocks, own_blocks,
-    footprints, table, temporal, row_factor, column, owner, sounding, flux_step,
-    departure, entries, live_count, error_id,
-    held, table_at, rows_at, mix_f, mix_b, wide_f, wide_b, base, place, step_of,
-    factor, column_at, owner_at, sounding_at, flux_at, departure_at, sems,
+    footprints, probes, table, temporal, row_factor, column, owner, sounding, flux_step,
+    departure, counts,
+    held, turned, own, table_at, rows_at, mix_f, mix_b, wide_f, wide_b, base, place, step_of,
+    factor, column_at, owner_at, sounding_at, flux_at, departure_at, counts_at,
+    sems, held_sems,
 ):
+    slots = place.shape[0]
+    block_rows = base.shape[1]
     pairs = [
         (temporal, factor), (column, column_at), (departure, departure_at), (owner, owner_at),
-        (sounding, sounding_at), (flux_step, flux_at), (row_factor, rows_at),
-        (table, table_at), (footprints, held),
+        (sounding, sounding_at), (flux_step, flux_at), (counts, counts_at), (row_factor, rows_at),
+        (table, table_at), (probes, own),
     ]
     copies = [pltpu.make_async_copy(a, b, sems.at[n]) for n, (a, b) in enumerate(pairs)]
+    fetches = []
+    for e in range(slots):
+        rows = pl.ds(e * block_rows, block_rows)
+        fetches.append(
+            pltpu.make_async_copy(footprints.at[rows], held.at[rows], held_sems.at[e])
+        )
+    for copy in copies + fetches:
+        copy.start()
     for copy in copies:
-        copy.start()
-    for copy in copies[:-2]:
         copy.wait()
     group = lax.axis_index("tm")
     mix_f[...] = mixing(factor, group, groups, steps, count, True)
@@ -89,23 +98,25 @@
     wide_f[...] = widen(column_at[...].T)
     wide_b[...] = widen(column_at[...])
     base[...] = jnp.zeros_like(base)
-    block_rows = base.shape[1]
     for q in range(own_blocks):
         at = (lax.axis_index("tile") * groups + group) * own_blocks + q
         base[pl.ds(pl.multiple_of(at * count, count), count), :] = jnp.broadcast_to(
             -departure_at[q : q + 1, :], (count, block_rows)
         )
         base[pl.ds(blocks * count + at, 1), :] = jnp.full(
-            (1, block_rows), live_count[q].astype(F32)
+            (1, block_rows), counts_at[1 + q].astype(F32)
         )
         base[pl.ds(blocks * count + blocks + at, 1), :] = jnp.full(
-            (1, block_rows), error_id[q].astype(F32)
-        )
-    for e in range(place.shape[0]):
+            (1, block_rows), counts_at[1 + own_blocks + q].astype(F32)
+        )
+    for e in range(slots):
         place[e] = owner_at[e] * (groups * own_blocks) + sounding_at[e]
-        step_of[e] = jnp.where(e < entries[0], flux_at[e], steps)
-    for copy in copies[-2:]:
-        copy.wait()
+        step_of[e] = jnp.where(e < counts_at[0], flux_at[e], steps)
+    for e in range(slots):
+        fetches[e].wait()
+        turned[:, e * block_rows : (e + 1) * block_rows] = held[
+            e * block_rows : (e + 1) * block_rows, :
+        ].T
 
 
 def row_mix(field, row_factor, transposed, wide, place):
@@ -129,28 +140,17 @@
 
 def predict_kernel(groups, steps, count, *refs):
     fields = refs[:groups]
-    (
-        mix_f, row_factor, wide_f, held, base, place, step_of, total,
-        mixed, fluxes,
-    ) = refs[groups:]
-    slots = place.shape[0]
+    mix_f, row_factor, wide_f, turned, base, place, step_of, total, mixed, fluxes = refs[groups:]
     block_rows = base.shape[1]
-    stacked = jnp.concatenate(
-        [fields[0][...]] + [f[...].reshape(fields[0].shape) for f in fields[1:]], axis=0
-    )
+    stacked = jnp.concatenate([f[...].reshape(mixed.shape) for f in fields], axis=0)
     both = jnp.dot(mix_f[...], stacked, preferred_element_type=F32)
     size = steps * count
     mixed[...] = both[:size] + both[size:]
     row_mix(mixed, row_factor, False, wide_f[...], fluxes)
     total[...] = base[...]
-    flux = fluxes[...]
-    for e in range(slots):
-        part = lax.dot_general(
-            flux,
-            held[e * block_rows : (e + 1) * block_rows, :],
-            (((1,), (1,)), ((), ())),
-            preferred_element_type=F32,
-        )
+    parts = jnp.dot(fluxes[...], turned[...], preferred_element_type=F32)
+    for e in range(place.shape[0]):
+        part = parts[:, e * block_rows : (e + 1) * block_rows]
         chosen = jnp.zeros((count, block_rows), F32)
         for t in range(steps):
             chosen = jnp.where(step_of[e] == t, part[t * count : (t + 1) * count], chosen)
@@ -189,8 +189,10 @@
     probes, mix_b, out = refs[groups:]
     stacked = jnp.concatenate([b[...] for b in backs], axis=0)
     both = jnp.dot(mix_b[...], stacked, preferred_element_type=F32)
-    size = out.shape[0]
-    out[...] = (probes[...].astype(F32) + (both[:size] + both[size:])).astype(BF16)
+    size = both.shape[0] // 2
+    before = probes[...].reshape(size, both.shape[1]).astype(F32)
+    after = (before + (both[:size] + both[size:])).astype(BF16)
+    out[...] = after.reshape(out.shape)
 
 
 def exchange(value, axis, distance):
@@ -202,7 +204,7 @@
     choices = [[]]
     for span in spans:
         choices = choices + [c + [span] for c in choices]
-    return choices[:0:-1]
+    return choices[1:]
 
 
 def hop(value, moves):
@@ -229,6 +231,10 @@
 
 def outside(*values):
     return [pltpu.with_memory_space_constraint(x, pltpu.HBM) for x in values]
+
+
+def inside(*values):
+    return [pltpu.with_memory_space_constraint(x, pltpu.VMEM) for x in values]
 
 
 def per_device(
@@ -255,45 +261,50 @@
     params = pltpu.CompilerParams(vmem_limit_bytes=VMEM_LIMIT)
 
     peers = [exchange(probes, "tm", d) for d in range(1, groups)]
-    own = probes.reshape(size, cells)
-    held, table, rows, mix_f, mix_b, wide_f, wide_b, base, place, step_of = pl.pallas_call(
-        functools.partial(prepare_kernel, groups, steps, count, blocks, own_blocks),
-        out_shape=[
-            pltpu.VMEM((slots * block_rows, cells), BF16),
-            pltpu.VMEM(precision_table.shape, F32),
-            pltpu.SMEM(row_factor.shape, F32),
-            pltpu.VMEM((2 * size, groups * size), BF16),
-            pltpu.VMEM((2 * size, groups * size), BF16),
-            pltpu.VMEM((2 * LANES, 2 * LANES), BF16),
-            pltpu.VMEM((2 * LANES, 2 * LANES), BF16),
-            pltpu.VMEM((blocks * (count + 2), block_rows), F32),
-            pltpu.SMEM((slots,), jnp.int32),
-            pltpu.SMEM((slots,), jnp.int32),
-        ],
-        in_specs=[in_hbm] * 9 + [in_smem] * 3,
-        out_specs=[in_vmem] * 2 + [in_smem] + [in_vmem] * 5 + [in_smem] * 2,
-        scratch_shapes=[
-            pltpu.SMEM(temporal_factor.shape, F32),
-            pltpu.VMEM(column_factor.shape, F32),
-            pltpu.SMEM((slots,), jnp.int32),
-            pltpu.SMEM((slots,), jnp.int32),
-            pltpu.SMEM((slots,), jnp.int32),
-            pltpu.VMEM(departure.shape, F32),
-            pltpu.SemaphoreType.DMA((9,)),
-        ],
-        compiler_params=params,
-        name="prepare",
-    )(
-        *outside(
-            footprints.reshape(slots * block_rows, cells), precision_table, temporal_factor, row_factor, column_factor,
-            owner_tile.reshape(slots), sounding_index, flux_step, departure,
-        ),
-        entry_count, live_count, error_id,
-    )
-    held, table, mix_f, mix_b, wide_f, wide_b, base = [
-        pltpu.with_memory_space_constraint(x, pltpu.VMEM)
-        for x in (held, table, mix_f, mix_b, wide_f, wide_b, base)
-    ]
+    held, turned, own, table, rows, mix_f, mix_b, wide_f, wide_b, base, place, step_of = (
+        pl.pallas_call(
+            functools.partial(prepare_kernel, groups, steps, count, blocks, own_blocks),
+            out_shape=[
+                pltpu.VMEM((slots * block_rows, cells), BF16),
+                pltpu.VMEM((cells, slots * block_rows), BF16),
+                pltpu.VMEM(probes.shape, BF16),
+                pltpu.VMEM(precision_table.shape, F32),
+                pltpu.SMEM(row_factor.shape, F32),
+                pltpu.VMEM((2 * size, groups * size), BF16),
+                pltpu.VMEM((2 * size, groups * size), BF16),
+                pltpu.VMEM((2 * LANES, 2 * LANES), BF16),
+                pltpu.VMEM((2 * LANES, 2 * LANES), BF16),
+                pltpu.VMEM((blocks * (count + 2), block_rows), F32),
+                pltpu.SMEM((slots,), jnp.int32),
+                pltpu.SMEM((slots,), jnp.int32),
+            ],
+            in_specs=[in_hbm] * 11,
+            out_specs=[in_vmem] * 4 + [in_smem] + [in_vmem] * 5 + [in_smem] * 2,
+            scratch_shapes=[
+                pltpu.SMEM(temporal_factor.shape, F32),
+                pltpu.VMEM(column_factor.shape, F32),
+                pltpu.SMEM((slots,), jnp.int32),
+                pltpu.SMEM((slots,), jnp.int32),
+                pltpu.SMEM((slots,), jnp.int32),
+                pltpu.VMEM(departure.shape, F32),
+                pltpu.SMEM((1 + 2 * own_blocks,), jnp.int32),
+                pltpu.SemaphoreType.DMA((10,)),
+                pltpu.SemaphoreType.DMA((slots,)),
+            ],
+            compiler_params=params,
+            name="prepare",
+        )(
+            *outside(
+                footprints.reshape(slots * block_rows, cells), probes, precision_table,
+                temporal_factor, row_factor, column_factor, owner_tile.reshape(slots),
+                sounding_index, flux_step, departure,
+            ),
+            jnp.concatenate([entry_count, live_count, error_id]),
+        )
+    )
+    held, turned, own, table, mix_f, mix_b, wide_f, wide_b, base = inside(
+        held, turned, own, table, mix_f, mix_b, wide_f, wide_b, base
+    )
 
     total = pl.pallas_call(
         functools.partial(predict_kernel, groups, steps, count),
@@ -306,10 +317,7 @@
         ],
         compiler_params=params,
         name="predict",
-    )(
-        own, *peers,
-        mix_f, rows, wide_f, held, base, place, step_of,
-    )
+    )(own, *peers, mix_f, rows, wide_f, turned, base, place, step_of)
     total = everywhere(total)
 
     back = pl.pallas_call(
@@ -326,15 +334,14 @@
     )(total, table, rows, wide_b, held, place, step_of)
 
     backs = [back] + [exchange(back, "tm", d) for d in range(1, groups)]
-    result = pl.pallas_call(
+    return pl.pallas_call(
         functools.partial(finish_kernel, groups),
-        out_shape=jax.ShapeDtypeStruct((size, cells), BF16),
+        out_shape=jax.ShapeDtypeStruct(probes.shape, BF16),
         in_specs=[in_vmem] * (groups + 2),
         out_specs=in_vmem,
         compiler_params=params,
         name="finish",
     )(*backs, own, mix_b)
-    return result.reshape(count, steps, cells)
 
 
 def solution(mesh):

time: 35.6 us -> 33.3 us (0.935)
  Pallas kernels: 6.47 us -> 8.46 us
  local copies, waits for them, and re-layouts: 1.97 us -> 0 us
  waiting for transfers between devices: 14.4 us -> 13 us
  starting transfers between devices: 10.5 us -> 9.5 us
    reshape x2 -> x0, local copies, waits for them, and re-layouts: 1.97 us -> none  [the longest x1 1.08 us: per_device(): own = probes.reshape(size, cells)]
    pallas_call x1, Pallas kernels: 2.42 us -> 4.17 us  [per_device(): pl.pallas_call(functools.partial(prepare_kernel, groups, steps, count, bl...]
    ppermute x4, waiting for transfers between devices: 7.65 us -> 6.64 us  [hop(): lax.ppermute(value, ('tile', 'tm'), [(i, i ^ flip) for i in range(tiles *...]
    pallas_call x1, Pallas kernels: 0.28 us -> 1.07 us  [per_device(): pl.pallas_call(functools.partial(finish_kernel, groups), out_shape=jax.Sh...]
    ppermute x4, starting transfers between devices: 6.84 us -> 6.21 us  [hop(): lax.ppermute(value, ('tile', 'tm'), [(i, i ^ flip) for i in range(tiles *...]
    pallas_call x1, Pallas kernels: 2.26 us -> 1.66 us  [per_device(): pl.pallas_call(functools.partial(predict_kernel, groups, steps, count), o...]
    ppermute x2, waiting for transfers between devices: 6.78 us -> 6.4 us  [exchange(): return lax.ppermute(value, axis, [(i, i ^ distance) for i in range(size)])]
    ppermute x2, starting transfers between devices: 3.66 us -> 3.29 us  [exchange(): return lax.ppermute(value, axis, [(i, i ^ distance) for i in range(size)])]
  transfers between devices with their start and end apart: 6 -> 6, of which waited for: 6 -> 6; matrix products, arithmetic and copies ran while one was open for 3% -> 0% of each run, Pallas kernels for 7% -> 13%
where the time goes in v2:
time: 33.3 us; the launch traced here: 33.2 us
  waiting for transfers between devices  13 us (39%)
  starting transfers between devices  9.5 us (29%)
  Pallas kernels  8.46 us (25%)
  between operations  1.98 us (6%)
    ppermute x4, waiting for transfers between devices, hop(): lax.ppermute(value, ('tile', 'tm'), [(i, i ^ flip) for i in range(tiles *...  6.64 us
    ppermute x2, waiting for transfers between devices, exchange(): return lax.ppermute(value, axis, [(i, i ^ distance) for i in range(size)])  6.4 us
    ppermute x4, starting transfers between devices, hop(): lax.ppermute(value, ('tile', 'tm'), [(i, i ^ flip) for i in range(tiles *...  6.21 us
    pallas_call x1, Pallas kernels, per_device(): pl.pallas_call(functools.partial(prepare_kernel, groups, steps, count, bl...  4.17 us
    ppermute x2, starting transfers between devices, exchange(): return lax.ppermute(value, axis, [(i, i ^ distance) for i in range(size)])  3.29 us
    pallas_call x1, Pallas kernels, per_device(): pl.pallas_call(functools.partial(predict_kernel, groups, steps, count), o...  1.66 us
    pallas_call x1, Pallas kernels, per_device(): pl.pallas_call(functools.partial(adjoint_kernel, steps, count, blocks), o...  1.57 us
    pallas_call x1, Pallas kernels, per_device(): pl.pallas_call(functools.partial(finish_kernel, groups), out_shape=jax.Sh...  1.07 us
  transfers between devices with their start and end apart: 6, of which 6 were waited for; matrix products, arithmetic and copies ran while one was open for 0% of the time, Pallas kernels for 13%

profile of v2, /device:TPU:0, one launch (start us, length us, event | category | flops | bytes accessed | tf_op | source)
XLA Modules:
  0.0 33.2 jit_solution(370626340933641176)
XLA Ops:
  0.0 2.9 %collective-permute-start = (bf16[32,2,2048]{2,1,0:T(2,128)(2,1)}, bf16[32,2,2048]{2,1,0:T(2,128)(2,1)S(1)}, u32[]{:S(2)}, u32[]{:S(2)}) collective-permute-start(bf16[32,2,2048]{2,1,0:T(2,128)(2,1)} %probes.1), channel_id=1, source_target_pairs={{0,2},{2,0},{1,3},{3,1},{4,6},{6,4},{5,7},{7,5},{8,10},{10,8},{9,1... | collective-permute-start | bytes 786440 | tf_op jit(solution)/shard_map/ppermute | solution.py:200
  4.9 0.1 pad_add_fusion.counts
  5.0 4.2 %prepare.1 = (bf16[1024,2048]{1,0:T(8,128)(2,1)S(1)}, bf16[2048,1024]{1,0:T(8,128)(2,1)S(1)}, bf16[32,2,2048]{2,1,0:T(2,128)(2,1)S(1)}, f32[4,128,128]{2,1,0:T(8...) custom-call(bf16[1024,2048]{1,0:T(8,128)(2,1)} %bitcast.2, ...), custom_call_target="tpu_custom_call" | custom-call | tf_op jit(solution)/shard_map/prepare/pallas_call | solution.py:265
  9.1 0.3 collective-permute-done.refs_1_
  9.5 1.7 %predict.1 = f32[272,128]{1,0:T(8,128)S(1)} custom-call(bf16[32,2,2048]{2,1,0:T(2,128)(2,1)S(1)} %get-tuple-element.17.refs_0_.refs_2_, bf16[32,2,2048]{2,1,0:T(2,128)(2,1)S(1)} %collective-permute-done.refs_1_, bf16[128,128]{1,0:T(8,128)(2,1)S(1)} %get-tuple-element.18.refs_2_, f32[16,16]{1,0:T(8,128)S(4)} %get-tuple-element.19.refs_3_.row_factor, ...), custom_call_target="tpu_custom_call" | custom-call | tf_op jit(solution)/shard_map/predict/pallas_call | solution.py:309
  11.1 2.8 %collective-permute-start.3 = (bf16[272,128]{1,0:T(8,128)(2,1)S(1)}, bf16[272,128]{1,0:T(8,128)(2,1)S(1)}, u32[]{:S(2)}, u32[]{:S(2)}) collective-permute-start(bf16[272,128]{1,0:T(8,128)(2,1)S(1)} %convert_element_type.18), channel_id=1, source_target_pairs={{0,6},{2,4},{4,2},{6,0},{8,14},{10,12},{12,10},{14,8},{1,7},{3,5},... | collective-permute-start | bytes 208904 | tf_op jit(solution)/shard_map/ppermute | solution.py:213
  14.0 0.4 %collective-permute-start.2 = (bf16[272,128]{1,0:T(8,128)(2,1)S(1)}, bf16[272,128]{1,0:T(8,128)(2,1)S(1)}, u32[]{:S(2)}, u32[]{:S(2)}) collective-permute-start(bf16[272,128]{1,0:T(8,128)(2,1)S(1)} %convert_element_type.18), channel_id=1, source_target_pairs={{0,4},{2,6},{4,0},{6,2},{8,12},{10,14},{12,8},{14,10},{1,5},{3,7},... | collective-permute-start | bytes 208904 | tf_op jit(solution)/shard_map/ppermute | solution.py:213
  14.4 0.3 collective-permute-start.1
  14.7 2.1 %collective-permute-done.3 = bf16[272,128]{1,0:T(8,128)(2,1)S(1)} collective-permute-done((bf16[272,128]{1,0:T(8,128)(2,1)S(1)}, bf16[272,128]{1,0:T(8,128)(2,1)S(1)}, u32[]{:S(2)}, u32[]{:S(2)}) %collective-permute-start.3) | collective-permute-done | bytes 69664 | tf_op jit(solution)/shard_map/ppermute | solution.py:213
  16.8 1.5 %collective-permute-done.2 = bf16[272,128]{1,0:T(8,128)(2,1)S(1)} collective-permute-done((bf16[272,128]{1,0:T(8,128)(2,1)S(1)}, bf16[272,128]{1,0:T(8,128)(2,1)S(1)}, u32[]{:S(2)}, u32[]{:S(2)}) %collective-permute-start.2) | collective-permute-done | bytes 69664 | tf_op jit(solution)/shard_map/ppermute | solution.py:213
  18.3 0.4 %collective-permute-done.1 = bf16[272,128]{1,0:T(8,128)(2,1)S(1)} collective-permute-done((bf16[272,128]{1,0:T(8,128)(2,1)S(1)}, bf16[272,128]{1,0:T(8,128)(2,1)S(1)}, u32[]{:S(2)}, u32[]{:S(2)}) %collective-permute-start.1) | collective-permute-done | bytes 69664 | tf_op jit(solution)/shard_map/ppermute | solution.py:213
  18.8 2.7 %collective-permute-start.4 = (bf16[272,128]{1,0:T(8,128)(2,1)S(1)}, bf16[272,128]{1,0:T(8,128)(2,1)S(1)}, u32[]{:S(2)}, u32[]{:S(2)}) collective-permute-start(bf16[272,128]{1,0:T(8,128)(2,1)S(1)} %fusion), channel_id=1, source_target_pairs={{0,8},{2,10},{4,12},{6,14},{8,0},{10,2},{12,4},{14,6},{1,9},{3,11}... | collective-permute-start | bytes 208904 | tf_op jit(solution)/shard_map/ppermute | solution.py:213
  21.4 2.6 %collective-permute-done.4 = bf16[272,128]{1,0:T(8,128)(2,1)S(1)} collective-permute-done((bf16[272,128]{1,0:T(8,128)(2,1)S(1)}, bf16[272,128]{1,0:T(8,128)(2,1)S(1)}, u32[]{:S(2)}, u32[]{:S(2)}) %collective-permute-start.4) | collective-permute-done | bytes 69664 | tf_op jit(solution)/shard_map/ppermute | solution.py:213
  24.1 1.6 %adjoint.1.refs_0_ = bf16[64,2048]{1,0:T(8,128)(2,1)S(1)} custom-call(f32[272,128]{1,0:T(8,128)S(1)} %convert_add_fusion.total, f32[4,128,128]{2,1,0:T(8,128)S(1)} %get-tuple-element.25.table, f32[16,16]{1,0:T(8,128)S(4)} %get-tuple-element.19.refs_3_.row_factor, bf16[256,256]{1,0:T(8,128)(2,1)S(1)} %get-tuple-element.26.wide_b, ...), custom_call_target="tpu_custom_call" | custom-call | tf_op jit(solution)/shard_map/adjoint/pallas_call | solution.py:323
  25.6 0.4 %collective-permute-start.5 = (bf16[64,2048]{1,0:T(8,128)(2,1)S(1)}, bf16[64,2048]{1,0:T(8,128)(2,1)S(1)}, u32[]{:S(2)}, u32[]{:S(2)}) collective-permute-start(bf16[64,2048]{1,0:T(8,128)(2,1)S(1)} %adjoint.1.refs_0_), channel_id=1, source_target_pairs={{0,2},{2,0},{1,3},{3,1},{4,6},{6,4},{5,7},{7,5},{8,10},{10,8},{9,1... | collective-permute-start | bytes 786440 | tf_op jit(solution)/shard_map/ppermute | solution.py:200
  26.0 6.1 %collective-permute-done.5.refs_1_ = bf16[64,2048]{1,0:T(8,128)(2,1)S(1)} collective-permute-done((bf16[64,2048]{1,0:T(8,128)(2,1)S(1)}, bf16[64,2048]{1,0:T(8,128)(2,1)S(1)}, u32[]{:S(2)}, u32[]{:S(2)}) %collective-permute-start.5) | collective-permute-done | bytes 262176 | tf_op jit(solution)/shard_map/ppermute | solution.py:200
  32.1 1.1 %finish.1 = bf16[32,2,2048]{2,1,0:T(2,128)(2,1)} custom-call(bf16[64,2048]{1,0:T(8,128)(2,1)S(1)} %adjoint.1.refs_0_, bf16[64,2048]{1,0:T(8,128)(2,1)S(1)} %collective-permute-done.5.refs_1_, bf16[32,2,2048]{2,1,0:T(2,128)(2,1)S(1)} %get-tuple-element.17.refs_0_.refs_2_, bf16[128,128]{1,0:T(8,128)(2,1)S(1)} %get-tuple-element.28.refs_3_), custom_call_target="tpu_custom_call" | custom-call | tf_op jit(solution)/shard_map/finish/pallas_call | solution.py:337
  (3 shorter events, 0.1 us)
Async XLA Ops:
  0.0 9.5 %collective-permute-start = (bf16[32,2,2048]{2,1,0:T(2,128)(2,1)}, bf16[32,2,2048]{2,1,0:T(2,128)(2,1)S(1)}, u32[]{:S(2)}, u32[]{:S(2)}) collective-permute-start(bf16[32,2,2048]{2,1,0:T(2,128)(2,1)} %probes.1), channel_id=1, source_target_pairs={{0,2},{2,0},{1,3},{3,1},{4,6},{6,4},{5,7},{7,5},{8,10},{10,8},{9,1... | collective-permute-start | bytes 786440 | tf_op jit(solution)/shard_map/ppermute | solution.py:200
  11.1 5.6 %collective-permute-start.3 = (bf16[272,128]{1,0:T(8,128)(2,1)S(1)}, bf16[272,128]{1,0:T(8,128)(2,1)S(1)}, u32[]{:S(2)}, u32[]{:S(2)}) collective-permute-start(bf16[272,128]{1,0:T(8,128)(2,1)S(1)} %convert_element_type.18), channel_id=1, source_target_pairs={{0,6},{2,4},{4,2},{6,0},{8,14},{10,12},{12,10},{14,8},{1,7},{3,5},... | collective-permute-start | bytes 208904 | tf_op jit(solution)/shard_map/ppermute | solution.py:213
  14.0 4.3 %collective-permute-start.2 = (bf16[272,128]{1,0:T(8,128)(2,1)S(1)}, bf16[272,128]{1,0:T(8,128)(2,1)S(1)}, u32[]{:S(2)}, u32[]{:S(2)}) collective-permute-start(bf16[272,128]{1,0:T(8,128)(2,1)S(1)} %convert_element_type.18), channel_id=1, source_target_pairs={{0,4},{2,6},{4,0},{6,2},{8,12},{10,14},{12,8},{14,10},{1,5},{3,7},... | collective-permute-start | bytes 208904 | tf_op jit(solution)/shard_map/ppermute | solution.py:213
  14.4 4.3 %collective-permute-start.1 = (bf16[272,128]{1,0:T(8,128)(2,1)S(1)}, bf16[272,128]{1,0:T(8,128)(2,1)S(1)}, u32[]{:S(2)}, u32[]{:S(2)}) collective-permute-start(bf16[272,128]{1,0:T(8,128)(2,1)S(1)} %convert_element_type.18), channel_id=1, source_target_pairs={{0,2},{2,0},{4,6},{6,4},{8,10},{10,8},{12,14},{14,12},{1,3},{3,1},... | collective-permute-start | bytes 208904 | tf_op jit(solution)/shard_map/ppermute | solution.py:213
  18.8 5.3 %collective-permute-start.4 = (bf16[272,128]{1,0:T(8,128)(2,1)S(1)}, bf16[272,128]{1,0:T(8,128)(2,1)S(1)}, u32[]{:S(2)}, u32[]{:S(2)}) collective-permute-start(bf16[272,128]{1,0:T(8,128)(2,1)S(1)} %fusion), channel_id=1, source_target_pairs={{0,8},{2,10},{4,12},{6,14},{8,0},{10,2},{12,4},{14,6},{1,9},{3,11}... | collective-permute-start | bytes 208904 | tf_op jit(solution)/shard_map/ppermute | solution.py:213
  25.6 6.4 %collective-permute-start.5 = (bf16[64,2048]{1,0:T(8,128)(2,1)S(1)}, bf16[64,2048]{1,0:T(8,128)(2,1)S(1)}, u32[]{:S(2)}, u32[]{:S(2)}) collective-permute-start(bf16[64,2048]{1,0:T(8,128)(2,1)S(1)} %adjoint.1.refs_0_), channel_id=1, source_target_pairs={{0,2},{2,0},{1,3},{3,1},{4,6},{6,4},{5,7},{7,5},{8,10},{10,8},{9,1... | collective-permute-start | bytes 786440 | tf_op jit(solution)/shard_map/ppermute | solution.py:200

commit v3 on v2

--- a/solution.py
+++ b/solution.py
@@ -90,6 +90,11 @@
         )
     for copy in copies + fetches:
         copy.start()
+    for e in range(slots):
+        fetches[e].wait()
+        turned[:, e * block_rows : (e + 1) * block_rows] = held[
+            e * block_rows : (e + 1) * block_rows, :
+        ].T
     for copy in copies:
         copy.wait()
     group = lax.axis_index("tm")
@@ -112,17 +117,12 @@
     for e in range(slots):
         place[e] = owner_at[e] * (groups * own_blocks) + sounding_at[e]
         step_of[e] = jnp.where(e < counts_at[0], flux_at[e], steps)
-    for e in range(slots):
-        fetches[e].wait()
-        turned[:, e * block_rows : (e + 1) * block_rows] = held[
-            e * block_rows : (e + 1) * block_rows, :
-        ].T
-
-
-def row_mix(field, row_factor, transposed, wide, place):
+
+
+def row_mix(field, row_factor, transposed, wide, place, first=0):
     rows = row_factor.shape[0]
     batch = 4
-    for start in range(0, rows, batch):
+    for start in range(first, first + place.shape[1] // LANES, batch):
         sums = [None] * batch
         for j in range(rows):
             tile = field[:, j * LANES : (j + 1) * LANES]
@@ -135,7 +135,7 @@
         size = sums[0].shape[0]
         for n in range(batch):
             i = start + n
-            place[:, i * LANES : (i + 1) * LANES] = result[n * size : (n + 1) * size]
+            place[:, (i - first) * LANES : (i - first + 1) * LANES] = result[n * size : (n + 1) * size]
 
 
 def predict_kernel(groups, steps, count, *refs):
@@ -161,7 +161,7 @@
 def adjoint_kernel(
     steps, count, blocks,
     total, table, row_factor, wide_b, held, place, step_of,
-    back, weights, adjoint,
+    back, adjoint, weights,
 ):
     block_rows = table.shape[1]
     slots = place.shape[0]
@@ -184,15 +184,22 @@
     row_mix(adjoint, row_factor, True, wide_b[...], back)
 
 
-def finish_kernel(groups, *refs):
+def adjoint_rest_kernel(first, adjoint, row_factor, wide_b, back):
+    row_mix(adjoint, row_factor, True, wide_b[...], back, first)
+
+
+def finish_kernel(groups, lanes, *refs):
     backs = refs[:groups]
-    probes, mix_b, out = refs[groups:]
+    probes, mix_b, *_, out, made, sem = refs[groups:]
     stacked = jnp.concatenate([b[...] for b in backs], axis=0)
     both = jnp.dot(mix_b[...], stacked, preferred_element_type=F32)
     size = both.shape[0] // 2
-    before = probes[...].reshape(size, both.shape[1]).astype(F32)
+    before = probes[:, :, lanes].reshape(size, both.shape[1]).astype(F32)
     after = (before + (both[:size] + both[size:])).astype(BF16)
-    out[...] = after.reshape(out.shape)
+    made[...] = after.reshape(made.shape)
+    copy = pltpu.make_async_copy(made, out.at[:, :, lanes], sem)
+    copy.start()
+    copy.wait()
 
 
 def exchange(value, axis, distance):
@@ -320,28 +327,48 @@
     )(own, *peers, mix_f, rows, wide_f, turned, base, place, step_of)
     total = everywhere(total)
 
-    back = pl.pallas_call(
+    half = cells // 2
+    low, adjoint = pl.pallas_call(
         functools.partial(adjoint_kernel, steps, count, blocks),
-        out_shape=jax.ShapeDtypeStruct((size, cells), BF16),
+        out_shape=[
+            jax.ShapeDtypeStruct((size, half), BF16),
+            jax.ShapeDtypeStruct((size, cells), F32),
+        ],
         in_specs=[in_vmem] * 2 + [in_smem] + [in_vmem] * 2 + [in_smem] * 2,
-        out_specs=in_vmem,
-        scratch_shapes=[
-            pltpu.VMEM((size, slots * block_rows), BF16),
-            pltpu.VMEM((size, cells), F32),
-        ],
+        out_specs=[in_vmem] * 2,
+        scratch_shapes=[pltpu.VMEM((size, slots * block_rows), BF16)],
         compiler_params=params,
         name="adjoint",
     )(total, table, rows, wide_b, held, place, step_of)
-
-    backs = [back] + [exchange(back, "tm", d) for d in range(1, groups)]
-    return pl.pallas_call(
-        functools.partial(finish_kernel, groups),
-        out_shape=jax.ShapeDtypeStruct(probes.shape, BF16),
-        in_specs=[in_vmem] * (groups + 2),
+    lows = [low] + [exchange(low, "tm", d) for d in range(1, groups)]
+    high = pl.pallas_call(
+        functools.partial(adjoint_rest_kernel, half // LANES),
+        out_shape=jax.ShapeDtypeStruct((size, cells - half), BF16),
+        in_specs=[in_vmem, in_smem, in_vmem],
         out_specs=in_vmem,
         compiler_params=params,
-        name="finish",
-    )(*backs, own, mix_b)
+        name="adjoint_rest",
+    )(adjoint, rows, wide_b)
+    highs = [high] + [exchange(high, "tm", d) for d in range(1, groups)]
+
+    made = []
+    for lanes, backs in ((slice(0, half), lows), (slice(half, cells), highs)):
+        made = [
+            pl.pallas_call(
+                functools.partial(finish_kernel, groups, lanes),
+                out_shape=jax.ShapeDtypeStruct(probes.shape, BF16),
+                in_specs=[in_vmem] * (groups + 2) + [in_hbm] * len(made),
+                out_specs=in_hbm,
+                input_output_aliases={groups + 2: 0} if made else {},
+                scratch_shapes=[
+                    pltpu.VMEM((count, steps, lanes.stop - lanes.start), BF16),
+                    pltpu.SemaphoreType.DMA,
+                ],
+                compiler_params=params,
+                name="finish",
+            )(*backs, own, mix_b, *made)
+        ]
+    return made[0]
 
 
 def solution(mesh):

time: 33.3 us -> 32.9 us (0.988)
  waiting for transfers between devices: 13 us -> 10.9 us
  starting transfers between devices: 9.5 us -> 11.3 us
    ppermute x2 -> x3, waiting for transfers between devices: 6.4 us -> 4.27 us  [exchange(): return lax.ppermute(value, axis, [(i, i ^ distance) for i in range(size)])]
    ppermute x2 -> x3, starting transfers between devices: 3.29 us -> 5.09 us  [exchange(): return lax.ppermute(value, axis, [(i, i ^ distance) for i in range(size)])]
    pallas_call x1 -> x3, Pallas kernels: 1.07 us -> 2.32 us  [the longest x2 1.87 us: per_device(): pl.pallas_call(functools.partial(finish_kernel, groups, lanes), out_shape...]
    pallas_call x1, Pallas kernels: 4.17 us -> 3.1 us  [per_device(): pl.pallas_call(functools.partial(prepare_kernel, groups, steps, count, bl...]
  transfers between devices with their start and end apart: 6 -> 7, of which waited for: 6 -> 7; matrix products, arithmetic and copies ran while one was open for 0% -> 0% of each run, Pallas kernels for 13% -> 14%
where the time goes in v3:
time: 32.9 us; the launch traced here: 32.8 us
  starting transfers between devices  11.3 us (34%)
  waiting for transfers between devices  10.9 us (33%)
  Pallas kernels  8.38 us (25%)
  between operations  2 us (6%)
    ppermute x4, waiting for transfers between devices, hop(): lax.ppermute(value, ('tile', 'tm'), [(i, i ^ flip) for i in range(tiles *...  6.64 us
    ppermute x4, starting transfers between devices, hop(): lax.ppermute(value, ('tile', 'tm'), [(i, i ^ flip) for i in range(tiles *...  6.21 us
    ppermute x3, starting transfers between devices, exchange(): return lax.ppermute(value, axis, [(i, i ^ distance) for i in range(size)])  5.09 us
    ppermute x3, waiting for transfers between devices, exchange(): return lax.ppermute(value, axis, [(i, i ^ distance) for i in range(size)])  4.27 us
    pallas_call x1, Pallas kernels, per_device(): pl.pallas_call(functools.partial(prepare_kernel, groups, steps, count, bl...  3.1 us
    pallas_call x2, Pallas kernels, per_device(): pl.pallas_call(functools.partial(finish_kernel, groups, lanes), out_shape...  1.87 us
    pallas_call x1, Pallas kernels, per_device(): pl.pallas_call(functools.partial(predict_kernel, groups, steps, count), o...  1.65 us
    pallas_call x1, Pallas kernels, per_device(): pl.pallas_call(functools.partial(adjoint_kernel, steps, count, blocks), o...  1.31 us
  transfers between devices with their start and end apart: 7, of which 7 were waited for; matrix products, arithmetic and copies ran while one was open for 0% of the time, Pallas kernels for 14%

profile of v3, /device:TPU:0, one launch (start us, length us, event | category | flops | bytes accessed | tf_op | source)
XLA Modules:
  0.0 32.8 jit_solution(11010572061883697842)
XLA Ops:
  0.0 2.9 %collective-permute-start = (bf16[32,2,2048]{2,1,0:T(2,128)(2,1)}, bf16[32,2,2048]{2,1,0:T(2,128)(2,1)S(1)}, u32[]{:S(2)}, u32[]{:S(2)}) collective-permute-start(bf16[32,2,2048]{2,1,0:T(2,128)(2,1)} %probes.1), channel_id=1, source_target_pairs={{0,2},{2,0},{1,3},{3,1},{4,6},{6,4},{5,7},{7,5},{8,10},{10,8},{9,1... | collective-permute-start | bytes 786440 | tf_op jit(solution)/shard_map/ppermute | solution.py:207
  4.9 0.1 pad_add_fusion.counts
  5.0 3.1 %prepare.1 = (bf16[1024,2048]{1,0:T(8,128)(2,1)S(1)}, bf16[2048,1024]{1,0:T(8,128)(2,1)S(1)}, bf16[32,2,2048]{2,1,0:T(2,128)(2,1)S(1)}, f32[4,128,128]{2,1,0:T(8...) custom-call(bf16[1024,2048]{1,0:T(8,128)(2,1)} %bitcast.2, ...), custom_call_target="tpu_custom_call" | custom-call | tf_op jit(solution)/shard_map/prepare/pallas_call | solution.py:272
  8.1 1.4 %collective-permute-done.refs_1_ = bf16[32,2,2048]{2,1,0:T(2,128)(2,1)S(1)} collective-permute-done((bf16[32,2,2048]{2,1,0:T(2,128)(2,1)}, bf16[32,2,2048]{2,1,0:T(2,128)(2,1)S(1)}, u32[]{:S(2)}, u32[]{:S(2)}) %collective-permute-start) | collective-permute-done | bytes 262176 | tf_op jit(solution)/shard_map/ppermute | solution.py:207
  9.5 1.7 %predict.1 = f32[272,128]{1,0:T(8,128)S(1)} custom-call(bf16[32,2,2048]{2,1,0:T(2,128)(2,1)S(1)} %get-tuple-element.19.refs_0_.refs_2_, bf16[32,2,2048]{2,1,0:T(2,128)(2,1)S(1)} %collective-permute-done.refs_1_, bf16[128,128]{1,0:T(8,128)(2,1)S(1)} %get-tuple-element.20.refs_2_, f32[16,16]{1,0:T(8,128)S(4)} %get-tuple-element.21.refs_3_.row_factor, ...), custom_call_target="tpu_custom_call" | custom-call | tf_op jit(solution)/shard_map/predict/pallas_call | solution.py:316
  11.1 2.8 %collective-permute-start.3 = (bf16[272,128]{1,0:T(8,128)(2,1)S(1)}, bf16[272,128]{1,0:T(8,128)(2,1)S(1)}, u32[]{:S(2)}, u32[]{:S(2)}) collective-permute-start(bf16[272,128]{1,0:T(8,128)(2,1)S(1)} %convert_element_type.18), channel_id=1, source_target_pairs={{0,6},{2,4},{4,2},{6,0},{8,14},{10,12},{12,10},{14,8},{1,7},{3,5},... | collective-permute-start | bytes 208904 | tf_op jit(solution)/shard_map/ppermute | solution.py:220
  14.0 0.4 %collective-permute-start.2 = (bf16[272,128]{1,0:T(8,128)(2,1)S(1)}, bf16[272,128]{1,0:T(8,128)(2,1)S(1)}, u32[]{:S(2)}, u32[]{:S(2)}) collective-permute-start(bf16[272,128]{1,0:T(8,128)(2,1)S(1)} %convert_element_type.18), channel_id=1, source_target_pairs={{0,4},{2,6},{4,0},{6,2},{8,12},{10,14},{12,8},{14,10},{1,5},{3,7},... | collective-permute-start | bytes 208904 | tf_op jit(solution)/shard_map/ppermute | solution.py:220
  14.4 0.3 collective-permute-start.1
  14.7 2.0 %collective-permute-done.3 = bf16[272,128]{1,0:T(8,128)(2,1)S(1)} collective-permute-done((bf16[272,128]{1,0:T(8,128)(2,1)S(1)}, bf16[272,128]{1,0:T(8,128)(2,1)S(1)}, u32[]{:S(2)}, u32[]{:S(2)}) %collective-permute-start.3) | collective-permute-done | bytes 69664 | tf_op jit(solution)/shard_map/ppermute | solution.py:220
  16.7 1.5 %collective-permute-done.2 = bf16[272,128]{1,0:T(8,128)(2,1)S(1)} collective-permute-done((bf16[272,128]{1,0:T(8,128)(2,1)S(1)}, bf16[272,128]{1,0:T(8,128)(2,1)S(1)}, u32[]{:S(2)}, u32[]{:S(2)}) %collective-permute-start.2) | collective-permute-done | bytes 69664 | tf_op jit(solution)/shard_map/ppermute | solution.py:220
  18.3 0.4 %collective-permute-done.1 = bf16[272,128]{1,0:T(8,128)(2,1)S(1)} collective-permute-done((bf16[272,128]{1,0:T(8,128)(2,1)S(1)}, bf16[272,128]{1,0:T(8,128)(2,1)S(1)}, u32[]{:S(2)}, u32[]{:S(2)}) %collective-permute-start.1) | collective-permute-done | bytes 69664 | tf_op jit(solution)/shard_map/ppermute | solution.py:220
  18.8 2.7 %collective-permute-start.4 = (bf16[272,128]{1,0:T(8,128)(2,1)S(1)}, bf16[272,128]{1,0:T(8,128)(2,1)S(1)}, u32[]{:S(2)}, u32[]{:S(2)}) collective-permute-start(bf16[272,128]{1,0:T(8,128)(2,1)S(1)} %fusion), channel_id=1, source_target_pairs={{0,8},{2,10},{4,12},{6,14},{8,0},{10,2},{12,4},{14,6},{1,9},{3,11}... | collective-permute-start | bytes 208904 | tf_op jit(solution)/shard_map/ppermute | solution.py:220
  21.4 2.6 %collective-permute-done.4 = bf16[272,128]{1,0:T(8,128)(2,1)S(1)} collective-permute-done((bf16[272,128]{1,0:T(8,128)(2,1)S(1)}, bf16[272,128]{1,0:T(8,128)(2,1)S(1)}, u32[]{:S(2)}, u32[]{:S(2)}) %collective-permute-start.4) | collective-permute-done | bytes 69664 | tf_op jit(solution)/shard_map/ppermute | solution.py:220
  24.1 1.3 %adjoint.1 = (bf16[64,1024]{1,0:T(8,128)(2,1)S(1)}, f32[64,2048]{1,0:T(8,128)S(1)}) custom-call(f32[272,128]{1,0:T(8,128)S(1)} %convert_add_fusion.total, f32[4,128,128]{2,1,0:T(8,128)S(1)} %get-tuple-element.27.table, f32[16,16]{1,0:T(8,128)S(4)} %get-tuple-element.21.refs_3_.row_factor, bf16[256,256]{1,0:T(8,128)(2,1)S(1)} %get-tuple-element.28.wide_b, ...), custom_call_target="tpu_custom_call" | custom-call | tf_op jit(solution)/shard_map/adjoint/pallas_call | solution.py:331
  25.4 0.4 %collective-permute-start.6 = (bf16[64,1024]{1,0:T(8,128)(2,1)S(1)}, bf16[64,1024]{1,0:T(8,128)(2,1)S(1)}, u32[]{:S(2)}, u32[]{:S(2)}) collective-permute-start(bf16[64,1024]{1,0:T(8,128)(2,1)S(1)} %get-tuple-element.32.refs_0_), channel_id=1, source_target_pairs={{0,2},{2,0},{1,3},{3,1},{4,6},{6,4},{5,7},{7,5},{8,10},{10,8},{9,1... | collective-permute-start | bytes 393224 | tf_op jit(solution)/shard_map/ppermute | solution.py:207
  25.7 0.5 %adjoint_rest.1.refs_0_ = bf16[64,1024]{1,0:T(8,128)(2,1)S(1)} custom-call(f32[64,2048]{1,0:T(8,128)S(1)} %get-tuple-element.30.adjoint, f32[16,16]{1,0:T(8,128)S(4)} %get-tuple-element.21.refs_3_.row_factor, bf16[256,256]{1,0:T(8,128)(2,1)S(1)} %get-tuple-element.28.wide_b), custom_call_target="tpu_custom_call" | custom-call | tf_op jit(solution)/shard_map/adjoint_rest/pallas_call | solution.py:344
  26.2 1.8 %collective-permute-start.5 = (bf16[64,1024]{1,0:T(8,128)(2,1)S(1)}, bf16[64,1024]{1,0:T(8,128)(2,1)S(1)}, u32[]{:S(2)}, u32[]{:S(2)}) collective-permute-start(bf16[64,1024]{1,0:T(8,128)(2,1)S(1)} %adjoint_rest.1.refs_0_), channel_id=1, source_target_pairs={{0,2},{2,0},{1,3},{3,1},{4,6},{6,4},{5,7},{7,5},{8,10},{10,8},{9,1... | collective-permute-start | bytes 393224 | tf_op jit(solution)/shard_map/ppermute | solution.py:207
  28.0 2.4 %collective-permute-done.6.refs_1_ = bf16[64,1024]{1,0:T(8,128)(2,1)S(1)} collective-permute-done((bf16[64,1024]{1,0:T(8,128)(2,1)S(1)}, bf16[64,1024]{1,0:T(8,128)(2,1)S(1)}, u32[]{:S(2)}, u32[]{:S(2)}) %collective-permute-start.6) | collective-permute-done | bytes 131104 | tf_op jit(solution)/shard_map/ppermute | solution.py:207
  30.4 0.9 %finish.2.refs_4_ = bf16[32,2,2048]{2,1,0:T(2,128)(2,1)} custom-call(bf16[64,1024]{1,0:T(8,128)(2,1)S(1)} %get-tuple-element.32.refs_0_, bf16[64,1024]{1,0:T(8,128)(2,1)S(1)} %collective-permute-done.6.refs_1_, bf16[32,2,2048]{2,1,0:T(2,128)(2,1)S(1)} %get-tuple-element.19.refs_0_.refs_2_, bf16[128,128]{1,0:T(8,128)(2,1)S(1)} %get-tuple-element.31.refs_3_), custom_call_target="tpu_custom_call" | custom-call | tf_op jit(solution)/shard_map/finish/pallas_call | solution.py:357
  31.4 0.5 %collective-permute-done.5.refs_1_ = bf16[64,1024]{1,0:T(8,128)(2,1)S(1)} collective-permute-done((bf16[64,1024]{1,0:T(8,128)(2,1)S(1)}, bf16[64,1024]{1,0:T(8,128)(2,1)S(1)}, u32[]{:S(2)}, u32[]{:S(2)}) %collective-permute-start.5) | collective-permute-done | bytes 131104 | tf_op jit(solution)/shard_map/ppermute | solution.py:207
  31.8 0.9 %finish.3 = bf16[32,2,2048]{2,1,0:T(2,128)(2,1)} custom-call(bf16[64,1024]{1,0:T(8,128)(2,1)S(1)} %adjoint_rest.1.refs_0_, bf16[64,1024]{1,0:T(8,128)(2,1)S(1)} %collective-permute-done.5.refs_1_, bf16[32,2,2048]{2,1,0:T(2,128)(2,1)S(1)} %get-tuple-element.19.refs_0_.refs_2_, ...), custom_call_target="tpu_custom_call", output_to_operand_aliasing={{}: (4, {})} | custom-call | tf_op jit(solution)/shard_map/finish/pallas_call | solution.py:357
  (3 shorter events, 0.1 us)
Async XLA Ops:
  0.0 9.5 %collective-permute-start = (bf16[32,2,2048]{2,1,0:T(2,128)(2,1)}, bf16[32,2,2048]{2,1,0:T(2,128)(2,1)S(1)}, u32[]{:S(2)}, u32[]{:S(2)}) collective-permute-start(bf16[32,2,2048]{2,1,0:T(2,128)(2,1)} %probes.1), channel_id=1, source_target_pairs={{0,2},{2,0},{1,3},{3,1},{4,6},{6,4},{5,7},{7,5},{8,10},{10,8},{9,1... | collective-permute-start | bytes 786440 | tf_op jit(solution)/shard_map/ppermute | solution.py:207
  11.1 5.6 %collective-permute-start.3 = (bf16[272,128]{1,0:T(8,128)(2,1)S(1)}, bf16[272,128]{1,0:T(8,128)(2,1)S(1)}, u32[]{:S(2)}, u32[]{:S(2)}) collective-permute-start(bf16[272,128]{1,0:T(8,128)(2,1)S(1)} %convert_element_type.18), channel_id=1, source_target_pairs={{0,6},{2,4},{4,2},{6,0},{8,14},{10,12},{12,10},{14,8},{1,7},{3,5},... | collective-permute-start | bytes 208904 | tf_op jit(solution)/shard_map/ppermute | solution.py:220
  14.0 4.3 %collective-permute-start.2 = (bf16[272,128]{1,0:T(8,128)(2,1)S(1)}, bf16[272,128]{1,0:T(8,128)(2,1)S(1)}, u32[]{:S(2)}, u32[]{:S(2)}) collective-permute-start(bf16[272,128]{1,0:T(8,128)(2,1)S(1)} %convert_element_type.18), channel_id=1, source_target_pairs={{0,4},{2,6},{4,0},{6,2},{8,12},{10,14},{12,8},{14,10},{1,5},{3,7},... | collective-permute-start | bytes 208904 | tf_op jit(solution)/shard_map/ppermute | solution.py:220
  14.4 4.3 %collective-permute-start.1 = (bf16[272,128]{1,0:T(8,128)(2,1)S(1)}, bf16[272,128]{1,0:T(8,128)(2,1)S(1)}, u32[]{:S(2)}, u32[]{:S(2)}) collective-permute-start(bf16[272,128]{1,0:T(8,128)(2,1)S(1)} %convert_element_type.18), channel_id=1, source_target_pairs={{0,2},{2,0},{4,6},{6,4},{8,10},{10,8},{12,14},{14,12},{1,3},{3,1},... | collective-permute-start | bytes 208904 | tf_op jit(solution)/shard_map/ppermute | solution.py:220
  18.8 5.3 %collective-permute-start.4 = (bf16[272,128]{1,0:T(8,128)(2,1)S(1)}, bf16[272,128]{1,0:T(8,128)(2,1)S(1)}, u32[]{:S(2)}, u32[]{:S(2)}) collective-permute-start(bf16[272,128]{1,0:T(8,128)(2,1)S(1)} %fusion), channel_id=1, source_target_pairs={{0,8},{2,10},{4,12},{6,14},{8,0},{10,2},{12,4},{14,6},{1,9},{3,11}... | collective-permute-start | bytes 208904 | tf_op jit(solution)/shard_map/ppermute | solution.py:220
  25.4 5.0 %collective-permute-start.6 = (bf16[64,1024]{1,0:T(8,128)(2,1)S(1)}, bf16[64,1024]{1,0:T(8,128)(2,1)S(1)}, u32[]{:S(2)}, u32[]{:S(2)}) collective-permute-start(bf16[64,1024]{1,0:T(8,128)(2,1)S(1)} %get-tuple-element.32.refs_0_), channel_id=1, source_target_pairs={{0,2},{2,0},{1,3},{3,1},{4,6},{6,4},{5,7},{7,5},{8,10},{10,8},{9,1... | collective-permute-start | bytes 393224 | tf_op jit(solution)/shard_map/ppermute | solution.py:207
  26.2 5.6 %collective-permute-start.5 = (bf16[64,1024]{1,0:T(8,128)(2,1)S(1)}, bf16[64,1024]{1,0:T(8,128)(2,1)S(1)}, u32[]{:S(2)}, u32[]{:S(2)}) collective-permute-start(bf16[64,1024]{1,0:T(8,128)(2,1)S(1)} %adjoint_rest.1.refs_0_), channel_id=1, source_target_pairs={{0,2},{2,0},{1,3},{3,1},{4,6},{6,4},{5,7},{7,5},{8,10},{10,8},{9,1... | collective-permute-start | bytes 393224 | tf_op jit(solution)/shard_map/ppermute | solution.py:207

commit v4 on v3

--- a/solution.py
+++ b/solution.py
@@ -66,11 +66,37 @@
     return jnp.concatenate(halves(value), axis=0)
 
 
+def unmixing(factor, group, other, steps, count):
+    block = steps * count
+    row = lax.broadcasted_iota(jnp.int32, (block, block), 0)
+    col = lax.broadcasted_iota(jnp.int32, (block, block), 1)
+    same = lax.div(row, steps) == lax.rem(col, count)
+    value = jnp.zeros((block, block), F32)
+    for a in range(steps):
+        for b in range(steps):
+            here = same & (lax.div(col, count) == a) & (lax.rem(row, steps) == b)
+            value = jnp.where(here, factor[group * steps + a, other * steps + b], value)
+    high, low = halves(value)
+    return jnp.concatenate(
+        [
+            jnp.concatenate([high, high], axis=1),
+            jnp.concatenate([low, jnp.zeros_like(low)], axis=1),
+        ],
+        axis=0,
+    )
+
+
+def unmix(matrix, stacked):
+    both = jnp.dot(matrix, stacked, preferred_element_type=F32)
+    size = both.shape[0] // 2
+    return both[:size] + both[size:]
+
+
 def prepare_kernel(
     groups, steps, count, blocks, own_blocks,
     footprints, probes, table, temporal, row_factor, column, owner, sounding, flux_step,
     departure, counts,
-    held, turned, own, table_at, rows_at, mix_f, mix_b, wide_f, wide_b, base, place, step_of,
+    held, turned, own, table_at, rows_at, mix_f, mix_b, unmix_b, wide_f, wide_b, base, place, step_of,
     factor, column_at, owner_at, sounding_at, flux_at, departure_at, counts_at,
     sems, held_sems,
 ):
@@ -100,6 +126,8 @@
     group = lax.axis_index("tm")
     mix_f[...] = mixing(factor, group, groups, steps, count, True)
     mix_b[...] = mixing(factor, group, groups, steps, count, False)
+    for other in range(groups):
+        unmix_b[other] = unmixing(factor, group, group ^ other, steps, count)
     wide_f[...] = widen(column_at[...].T)
     wide_b[...] = widen(column_at[...])
     base[...] = jnp.zeros_like(base)
@@ -131,16 +159,21 @@
                 scale = row_factor[j, i] if transposed else row_factor[i, j]
                 term = scale * tile
                 sums[n] = term if sums[n] is None else sums[n] + term
-        result = times_wide(jnp.concatenate(sums, axis=0), wide).astype(BF16)
+        result = times_wide(jnp.concatenate(sums, axis=0), wide)
         size = sums[0].shape[0]
+        pieces = [result.astype(BF16)] if place.shape[0] == size else halves(result)
         for n in range(batch):
-            i = start + n
-            place[:, (i - first) * LANES : (i - first + 1) * LANES] = result[n * size : (n + 1) * size]
+            at = (start + n - first) * LANES
+            for m, piece in enumerate(pieces):
+                place[m * size : (m + 1) * size, at : at + LANES] = piece[n * size : (n + 1) * size]
 
 
 def predict_kernel(groups, steps, count, *refs):
     fields = refs[:groups]
-    mix_f, row_factor, wide_f, turned, base, place, step_of, total, mixed, fluxes = refs[groups:]
+    (
+        mix_f, row_factor, wide_f, turned, base, place, step_of,
+        total, sent, mixed, fluxes,
+    ) = refs[groups:]
     block_rows = base.shape[1]
     stacked = jnp.concatenate([f[...].reshape(mixed.shape) for f in fields], axis=0)
     both = jnp.dot(mix_f[...], stacked, preferred_element_type=F32)
@@ -156,13 +189,15 @@
             chosen = jnp.where(step_of[e] == t, part[t * count : (t + 1) * count], chosen)
         at = pl.ds(pl.multiple_of(place[e] * count, count), count)
         total[at, :] = total[at, :] + chosen
+    sent[...] = total[...].astype(BF16)
 
 
 def adjoint_kernel(
     steps, count, blocks,
-    total, table, row_factor, wide_b, held, place, step_of,
-    back, adjoint, weights,
+    near, far, table, row_factor, wide_b, held, place, step_of,
+    back, adjoint, weights, total,
 ):
+    total[...] = near[...] + far[...].astype(F32)
     block_rows = table.shape[1]
     slots = place.shape[0]
     lane = lax.broadcasted_iota(jnp.int32, (1, block_rows), 1).astype(F32)
@@ -184,22 +219,38 @@
     row_mix(adjoint, row_factor, True, wide_b[...], back)
 
 
-def adjoint_rest_kernel(first, adjoint, row_factor, wide_b, back):
-    row_mix(adjoint, row_factor, True, wide_b[...], back, first)
-
-
-def finish_kernel(groups, lanes, *refs):
-    backs = refs[:groups]
-    probes, mix_b, *_, out, made, sem = refs[groups:]
-    stacked = jnp.concatenate([b[...] for b in backs], axis=0)
-    both = jnp.dot(mix_b[...], stacked, preferred_element_type=F32)
-    size = both.shape[0] // 2
-    before = probes[:, :, lanes].reshape(size, both.shape[1]).astype(F32)
-    after = (before + (both[:size] + both[size:])).astype(BF16)
-    made[...] = after.reshape(made.shape)
+def adjoint_rest_kernel(first, adjoint, row_factor, wide_b, unmix_b, *refs):
+    *sent, stacked = refs
+    row_mix(adjoint, row_factor, True, wide_b[...], stacked, first)
+    for n, z in enumerate(sent):
+        z[...] = unmix(unmix_b[n + 1], stacked[...]).astype(BF16)
+
+
+def own_kernel(lanes, probes, stacked, unmix_b, out):
+    before = probes[:, :, lanes].reshape(out.shape).astype(F32)
+    out[...] = before + unmix(unmix_b[0], stacked[...])
+
+
+def put(value, made, out, lanes, sem):
+    made[...] = value.astype(BF16).reshape(made.shape)
     copy = pltpu.make_async_copy(made, out.at[:, :, lanes], sem)
     copy.start()
     copy.wait()
+
+
+def finish_low_kernel(groups, lanes, *refs):
+    backs = refs[:groups]
+    probes, mix_b, out, made, sem = refs[groups:]
+    mixed = unmix(mix_b[...], jnp.concatenate([b[...] for b in backs], axis=0))
+    put(probes[:, :, lanes].reshape(mixed.shape).astype(F32) + mixed, made, out, lanes, sem)
+
+
+def finish_high_kernel(lanes, *refs):
+    own, *sent, _, out, made, sem = refs
+    value = own[...]
+    for z in sent:
+        value = value + z[...].astype(F32)
+    put(value, made, out, lanes, sem)
 
 
 def exchange(value, axis, distance):
@@ -222,18 +273,21 @@
     )
 
 
-def everywhere(value):
+def everywhere(value, sent):
     spans = [
         (axis, 1 << n)
         for axis in ("tm", "tile")
         for n in range(lax.axis_size(axis).bit_length() - 1)
     ]
-    for start in range(0, len(spans), 2):
+    *terms, last = [hop(sent, moves) for moves in subsets(spans[:2])]
+    for start in range(2, len(spans), 2):
+        for term in terms + [last]:
+            value = value + term.astype(F32)
         sent = value.astype(BF16)
-        terms = [hop(sent, moves) for moves in subsets(spans[start : start + 2])]
-        for term in terms:
-            value = value + term.astype(F32)
-    return value
+        *terms, last = [hop(sent, moves) for moves in subsets(spans[start : start + 2])]
+    for term in terms:
+        value = value + term.astype(F32)
+    return value, last
 
 
 def outside(*values):
@@ -268,7 +322,7 @@
     params = pltpu.CompilerParams(vmem_limit_bytes=VMEM_LIMIT)
 
     peers = [exchange(probes, "tm", d) for d in range(1, groups)]
-    held, turned, own, table, rows, mix_f, mix_b, wide_f, wide_b, base, place, step_of = (
+    held, turned, own, table, rows, mix_f, mix_b, unmix_b, wide_f, wide_b, base, place, step_of = (
         pl.pallas_call(
             functools.partial(prepare_kernel, groups, steps, count, blocks, own_blocks),
             out_shape=[
@@ -279,6 +333,7 @@
                 pltpu.SMEM(row_factor.shape, F32),
                 pltpu.VMEM((2 * size, groups * size), BF16),
                 pltpu.VMEM((2 * size, groups * size), BF16),
+                pltpu.VMEM((groups, 2 * size, 2 * size), BF16),
                 pltpu.VMEM((2 * LANES, 2 * LANES), BF16),
                 pltpu.VMEM((2 * LANES, 2 * LANES), BF16),
                 pltpu.VMEM((blocks * (count + 2), block_rows), F32),
@@ -286,7 +341,7 @@
                 pltpu.SMEM((slots,), jnp.int32),
             ],
             in_specs=[in_hbm] * 11,
-            out_specs=[in_vmem] * 4 + [in_smem] + [in_vmem] * 5 + [in_smem] * 2,
+            out_specs=[in_vmem] * 4 + [in_smem] + [in_vmem] * 6 + [in_smem] * 2,
             scratch_shapes=[
                 pltpu.SMEM(temporal_factor.shape, F32),
                 pltpu.VMEM(column_factor.shape, F32),
@@ -309,15 +364,18 @@
             jnp.concatenate([entry_count, live_count, error_id]),
         )
     )
-    held, turned, own, table, mix_f, mix_b, wide_f, wide_b, base = inside(
-        held, turned, own, table, mix_f, mix_b, wide_f, wide_b, base
-    )
-
-    total = pl.pallas_call(
+    held, turned, own, table, mix_f, mix_b, unmix_b, wide_f, wide_b, base = inside(
+        held, turned, own, table, mix_f, mix_b, unmix_b, wide_f, wide_b, base
+    )
+
+    total, sent = pl.pallas_call(
         functools.partial(predict_kernel, groups, steps, count),
-        out_shape=jax.ShapeDtypeStruct(base.shape, F32),
+        out_shape=[
+            jax.ShapeDtypeStruct(base.shape, F32),
+            jax.ShapeDtypeStruct(base.shape, BF16),
+        ],
         in_specs=[in_vmem] * (groups + 1) + [in_smem] + [in_vmem] * 3 + [in_smem] * 2,
-        out_specs=in_vmem,
+        out_specs=[in_vmem] * 2,
         scratch_shapes=[
             pltpu.VMEM((size, cells), F32),
             pltpu.VMEM((size, cells), BF16),
@@ -325,7 +383,7 @@
         compiler_params=params,
         name="predict",
     )(own, *peers, mix_f, rows, wide_f, turned, base, place, step_of)
-    total = everywhere(total)
+    near, far = everywhere(total, sent)
 
     half = cells // 2
     low, adjoint = pl.pallas_call(
@@ -334,41 +392,55 @@
             jax.ShapeDtypeStruct((size, half), BF16),
             jax.ShapeDtypeStruct((size, cells), F32),
         ],
-        in_specs=[in_vmem] * 2 + [in_smem] + [in_vmem] * 2 + [in_smem] * 2,
+        in_specs=[in_vmem] * 3 + [in_smem] + [in_vmem] * 2 + [in_smem] * 2,
         out_specs=[in_vmem] * 2,
-        scratch_shapes=[pltpu.VMEM((size, slots * block_rows), BF16)],
+        scratch_shapes=[
+            pltpu.VMEM((size, slots * block_rows), BF16),
+            pltpu.VMEM(base.shape, F32),
+        ],
         compiler_params=params,
         name="adjoint",
-    )(total, table, rows, wide_b, held, place, step_of)
+    )(near, far, table, rows, wide_b, held, place, step_of)
     lows = [low] + [exchange(low, "tm", d) for d in range(1, groups)]
+    *sent, stacked = pl.pallas_call(
+        functools.partial(adjoint_rest_kernel, half // LANES),
+        out_shape=[jax.ShapeDtypeStruct((size, half), BF16)] * (groups - 1)
+        + [jax.ShapeDtypeStruct((2 * size, half), BF16)],
+        in_specs=[in_vmem, in_smem, in_vmem, in_vmem],
+        out_specs=[in_vmem] * groups,
+        compiler_params=params,
+        name="adjoint_rest",
+    )(adjoint, rows, wide_b, unmix_b)
+    highs = [exchange(z, "tm", d + 1) for d, z in enumerate(sent)]
+    low_lanes, high_lanes = slice(0, half), slice(half, cells)
     high = pl.pallas_call(
-        functools.partial(adjoint_rest_kernel, half // LANES),
-        out_shape=jax.ShapeDtypeStruct((size, cells - half), BF16),
-        in_specs=[in_vmem, in_smem, in_vmem],
+        functools.partial(own_kernel, high_lanes),
+        out_shape=jax.ShapeDtypeStruct((size, half), F32),
+        in_specs=[in_vmem] * 3,
         out_specs=in_vmem,
         compiler_params=params,
-        name="adjoint_rest",
-    )(adjoint, rows, wide_b)
-    highs = [high] + [exchange(high, "tm", d) for d in range(1, groups)]
-
-    made = []
-    for lanes, backs in ((slice(0, half), lows), (slice(half, cells), highs)):
-        made = [
-            pl.pallas_call(
-                functools.partial(finish_kernel, groups, lanes),
-                out_shape=jax.ShapeDtypeStruct(probes.shape, BF16),
-                in_specs=[in_vmem] * (groups + 2) + [in_hbm] * len(made),
-                out_specs=in_hbm,
-                input_output_aliases={groups + 2: 0} if made else {},
-                scratch_shapes=[
-                    pltpu.VMEM((count, steps, lanes.stop - lanes.start), BF16),
-                    pltpu.SemaphoreType.DMA,
-                ],
-                compiler_params=params,
-                name="finish",
-            )(*backs, own, mix_b, *made)
-        ]
-    return made[0]
+        name="own",
+    )(own, stacked, unmix_b)
+    scratch = [pltpu.VMEM((count, steps, half), BF16), pltpu.SemaphoreType.DMA]
+    made = pl.pallas_call(
+        functools.partial(finish_low_kernel, groups, low_lanes),
+        out_shape=jax.ShapeDtypeStruct(probes.shape, BF16),
+        in_specs=[in_vmem] * (groups + 2),
+        out_specs=in_hbm,
+        scratch_shapes=scratch,
+        compiler_params=params,
+        name="finish_low",
+    )(*lows, own, mix_b)
+    return pl.pallas_call(
+        functools.partial(finish_high_kernel, high_lanes),
+        out_shape=jax.ShapeDtypeStruct(probes.shape, BF16),
+        in_specs=[in_vmem] * groups + [in_hbm],
+        out_specs=in_hbm,
+        input_output_aliases={groups: 0},
+        scratch_shapes=scratch,
+        compiler_params=params,
+        name="finish_high",
+    )(high, *highs, made)
 
 
 def solution(mesh):

time: 32.9 us -> 32.7 us (level)
  waiting for transfers between devices: 10.9 us -> 10.4 us
    ppermute x3, waiting for transfers between devices: 4.27 us -> 3.74 us  [exchange(): return lax.ppermute(value, axis, [(i, i ^ distance) for i in range(size)])]
    pallas_call x2 -> x3, Pallas kernels: 1.87 us -> 1.87 us  [the longest x1 0.93 us: per_device(): pl.pallas_call(functools.partial(finish_low_kernel, groups, low_lanes), o...]
  transfers between devices with their start and end apart: 7 -> 7, of which waited for: 7 -> 7; matrix products, arithmetic and copies ran while one was open for 0% -> 0% of each run, Pallas kernels for 14% -> 15%
where the time goes in v4:
time: 32.7 us; the launch traced here: 32.5 us
  starting transfers between devices  11.3 us (35%)
  waiting for transfers between devices  10.4 us (32%)
  Pallas kernels  8.7 us (27%)
  between operations  2 us (6%)
    ppermute x4, waiting for transfers between devices, hop(): lax.ppermute(value, ('tile', 'tm'), [(i, i ^ flip) for i in range(tiles *...  6.62 us
    ppermute x4, starting transfers between devices, hop(): lax.ppermute(value, ('tile', 'tm'), [(i, i ^ flip) for i in range(tiles *...  6.21 us
    ppermute x3, starting transfers between devices, exchange(): return lax.ppermute(value, axis, [(i, i ^ distance) for i in range(size)])  5.09 us
    ppermute x3, waiting for transfers between devices, exchange(): return lax.ppermute(value, axis, [(i, i ^ distance) for i in range(size)])  3.74 us
    pallas_call x1, Pallas kernels, per_device(): pl.pallas_call(functools.partial(prepare_kernel, groups, steps, count, bl...  3.2 us
    pallas_call x1, Pallas kernels, per_device(): pl.pallas_call(functools.partial(predict_kernel, groups, steps, count), o...  1.67 us
    pallas_call x1, Pallas kernels, per_device(): pl.pallas_call(functools.partial(adjoint_kernel, steps, count, blocks), o...  1.32 us
    pallas_call x1, Pallas kernels, per_device(): pl.pallas_call(functools.partial(finish_low_kernel, groups, low_lanes), o...  0.93 us
  transfers between devices with their start and end apart: 7, of which 7 were waited for; matrix products, arithmetic and copies ran while one was open for 0% of the time, Pallas kernels for 15%

profile of v4, /device:TPU:0, one launch (start us, length us, event | category | flops | bytes accessed | tf_op | source)
XLA Modules:
  0.0 32.5 jit_solution(15186962364363221037)
XLA Ops:
  0.0 2.9 %collective-permute-start = (bf16[32,2,2048]{2,1,0:T(2,128)(2,1)}, bf16[32,2,2048]{2,1,0:T(2,128)(2,1)S(1)}, u32[]{:S(2)}, u32[]{:S(2)}) collective-permute-start(bf16[32,2,2048]{2,1,0:T(2,128)(2,1)} %probes.1), channel_id=1, source_target_pairs={{0,2},{2,0},{1,3},{3,1},{4,6},{6,4},{5,7},{7,5},{8,10},{10,8},{9,1... | collective-permute-start | bytes 786440 | tf_op jit(solution)/shard_map/ppermute | solution.py:258
  4.9 0.1 pad_add_fusion.counts
  5.0 3.2 %prepare.1 = (bf16[1024,2048]{1,0:T(8,128)(2,1)S(1)}, bf16[2048,1024]{1,0:T(8,128)(2,1)S(1)}, bf16[32,2,2048]{2,1,0:T(2,128)(2,1)S(1)}, f32[4,128,128]{2,1,0:T(8...) custom-call(bf16[1024,2048]{1,0:T(8,128)(2,1)} %bitcast.2, ...), custom_call_target="tpu_custom_call" | custom-call | tf_op jit(solution)/shard_map/prepare/pallas_call | solution.py:326
  8.2 1.3 %collective-permute-done.refs_1_ = bf16[32,2,2048]{2,1,0:T(2,128)(2,1)S(1)} collective-permute-done((bf16[32,2,2048]{2,1,0:T(2,128)(2,1)}, bf16[32,2,2048]{2,1,0:T(2,128)(2,1)S(1)}, u32[]{:S(2)}, u32[]{:S(2)}) %collective-permute-start) | collective-permute-done | bytes 262176 | tf_op jit(solution)/shard_map/ppermute | solution.py:258
  9.5 1.7 %predict.1 = (f32[272,128]{1,0:T(8,128)S(1)}, bf16[272,128]{1,0:T(8,128)(2,1)S(1)}) custom-call(bf16[32,2,2048]{2,1,0:T(2,128)(2,1)S(1)} %get-tuple-element.24.refs_0_.probes.refs_2_, bf16[32,2,2048]{2,1,0:T(2,128)(2,1)S(1)} %collective-permute-done.refs_1_, bf16[128,128]{1,0:T(8,128)(2,1)S(1)} %get-tuple-element.25.refs_2_, ...), custom_call_target="tpu_custom_call" | custom-call | tf_op jit(solution)/shard_map/predict/pallas_call | solution.py:371
  11.1 2.8 %collective-permute-start.3 = (bf16[272,128]{1,0:T(8,128)(2,1)S(1)}, bf16[272,128]{1,0:T(8,128)(2,1)S(1)}, u32[]{:S(2)}, u32[]{:S(2)}) collective-permute-start(bf16[272,128]{1,0:T(8,128)(2,1)S(1)} %get-tuple-element.33), channel_id=1, source_target_pairs={{0,6},{2,4},{4,2},{6,0},{8,14},{10,12},{12,10},{14,8},{1,7},{3,5},... | collective-permute-start | bytes 208904 | tf_op jit(solution)/shard_map/ppermute | solution.py:271
  14.0 0.4 %collective-permute-start.2 = (bf16[272,128]{1,0:T(8,128)(2,1)S(1)}, bf16[272,128]{1,0:T(8,128)(2,1)S(1)}, u32[]{:S(2)}, u32[]{:S(2)}) collective-permute-start(bf16[272,128]{1,0:T(8,128)(2,1)S(1)} %get-tuple-element.33), channel_id=1, source_target_pairs={{0,4},{2,6},{4,0},{6,2},{8,12},{10,14},{12,8},{14,10},{1,5},{3,7},... | collective-permute-start | bytes 208904 | tf_op jit(solution)/shard_map/ppermute | solution.py:271
  14.4 0.3 collective-permute-start.1
  14.7 2.0 %collective-permute-done.3 = bf16[272,128]{1,0:T(8,128)(2,1)S(1)} collective-permute-done((bf16[272,128]{1,0:T(8,128)(2,1)S(1)}, bf16[272,128]{1,0:T(8,128)(2,1)S(1)}, u32[]{:S(2)}, u32[]{:S(2)}) %collective-permute-start.3) | collective-permute-done | bytes 69664 | tf_op jit(solution)/shard_map/ppermute | solution.py:271
  16.7 1.5 %collective-permute-done.2 = bf16[272,128]{1,0:T(8,128)(2,1)S(1)} collective-permute-done((bf16[272,128]{1,0:T(8,128)(2,1)S(1)}, bf16[272,128]{1,0:T(8,128)(2,1)S(1)}, u32[]{:S(2)}, u32[]{:S(2)}) %collective-permute-start.2) | collective-permute-done | bytes 69664 | tf_op jit(solution)/shard_map/ppermute | solution.py:271
  18.3 0.4 %collective-permute-done.1 = bf16[272,128]{1,0:T(8,128)(2,1)S(1)} collective-permute-done((bf16[272,128]{1,0:T(8,128)(2,1)S(1)}, bf16[272,128]{1,0:T(8,128)(2,1)S(1)}, u32[]{:S(2)}, u32[]{:S(2)}) %collective-permute-start.1) | collective-permute-done | bytes 69664 | tf_op jit(solution)/shard_map/ppermute | solution.py:271
  18.7 2.7 %collective-permute-start.4 = (bf16[272,128]{1,0:T(8,128)(2,1)S(1)}, bf16[272,128]{1,0:T(8,128)(2,1)S(1)}, u32[]{:S(2)}, u32[]{:S(2)}) collective-permute-start(bf16[272,128]{1,0:T(8,128)(2,1)S(1)} %get-tuple-element.43), channel_id=1, source_target_pairs={{0,8},{2,10},{4,12},{6,14},{8,0},{10,2},{12,4},{14,6},{1,9},{3,11}... | collective-permute-start | bytes 208904 | tf_op jit(solution)/shard_map/ppermute | solution.py:271
  21.4 2.6 %collective-permute-done.4.far = bf16[272,128]{1,0:T(8,128)(2,1)S(1)} collective-permute-done((bf16[272,128]{1,0:T(8,128)(2,1)S(1)}, bf16[272,128]{1,0:T(8,128)(2,1)S(1)}, u32[]{:S(2)}, u32[]{:S(2)}) %collective-permute-start.4) | collective-permute-done | bytes 69664 | tf_op jit(solution)/shard_map/ppermute | solution.py:271
  24.0 1.3 %adjoint.1 = (bf16[64,1024]{1,0:T(8,128)(2,1)S(1)}, f32[64,2048]{1,0:T(8,128)S(1)}) custom-call(f32[272,128]{1,0:T(8,128)S(1)} %get-tuple-element.44.near, bf16[272,128]{1,0:T(8,128)(2,1)S(1)} %collective-permute-done.4.far, f32[4,128,128]{2,1,0:T(8,128)S(1)} %get-tuple-element.34.table, f32[16,16]{1,0:T(8,128)S(4)} %get-tuple-element.26.refs_3_.row_factor, ...), custom_call_target="tpu_custom_call" | custom-call | tf_op jit(solution)/shard_map/adjoint/pallas_call | solution.py:389
  25.3 0.4 %collective-permute-start.6 = (bf16[64,1024]{1,0:T(8,128)(2,1)S(1)}, bf16[64,1024]{1,0:T(8,128)(2,1)S(1)}, u32[]{:S(2)}, u32[]{:S(2)}) collective-permute-start(bf16[64,1024]{1,0:T(8,128)(2,1)S(1)} %get-tuple-element.41.refs_0_), channel_id=1, source_target_pairs={{0,2},{2,0},{1,3},{3,1},{4,6},{6,4},{5,7},{7,5},{8,10},{10,8},{9,1... | collective-permute-start | bytes 393224 | tf_op jit(solution)/shard_map/ppermute | solution.py:258
  25.7 0.6 %adjoint_rest.1 = (bf16[64,1024]{1,0:T(8,128)(2,1)S(1)}, bf16[128,1024]{1,0:T(8,128)(2,1)S(1)}) custom-call(f32[64,2048]{1,0:T(8,128)S(1)} %get-tuple-element.37.adjoint, f32[16,16]{1,0:T(8,128)S(4)} %get-tuple-element.26.refs_3_.row_factor, bf16[256,256]{1,0:T(8,128)(2,1)S(1)} %get-tuple-element.35.wide_b, bf16[2,128,128]{2,1,0:T(8,128)(2,1)S(1)} %get-tuple-element.38.unmix_b), custom_call_target="tpu_custom_call" | custom-call | tf_op jit(solution)/shard_map/adjoint_rest/pallas_call | solution.py:405
  26.4 1.8 %collective-permute-start.5 = (bf16[64,1024]{1,0:T(8,128)(2,1)S(1)}, bf16[64,1024]{1,0:T(8,128)(2,1)S(1)}, u32[]{:S(2)}, u32[]{:S(2)}) collective-permute-start(bf16[64,1024]{1,0:T(8,128)(2,1)S(1)} %get-tuple-element.40), channel_id=1, source_target_pairs={{0,2},{2,0},{1,3},{3,1},{4,6},{6,4},{5,7},{7,5},{8,10},{10,8},{9,1... | collective-permute-start | bytes 393224 | tf_op jit(solution)/shard_map/ppermute | solution.py:258
  28.1 0.2 own.1.refs_0_
  28.4 2.0 %collective-permute-done.6.refs_1_ = bf16[64,1024]{1,0:T(8,128)(2,1)S(1)} collective-permute-done((bf16[64,1024]{1,0:T(8,128)(2,1)S(1)}, bf16[64,1024]{1,0:T(8,128)(2,1)S(1)}, u32[]{:S(2)}, u32[]{:S(2)}) %collective-permute-start.6) | collective-permute-done | bytes 131104 | tf_op jit(solution)/shard_map/ppermute | solution.py:258
  30.4 0.9 %finish_low.1.refs_2_ = bf16[32,2,2048]{2,1,0:T(2,128)(2,1)} custom-call(bf16[64,1024]{1,0:T(8,128)(2,1)S(1)} %get-tuple-element.41.refs_0_, bf16[64,1024]{1,0:T(8,128)(2,1)S(1)} %collective-permute-done.6.refs_1_, bf16[32,2,2048]{2,1,0:T(2,128)(2,1)S(1)} %get-tuple-element.24.refs_0_.probes.refs_2_, bf16[128,128]{1,0:T(8,128)(2,1)S(1)} %get-tuple-element.42.refs_3_), custom_call_target="tpu_custom_call" | custom-call | tf_op jit(solution)/shard_map/finish_low/pallas_call | solution.py:425
  31.3 0.5 %collective-permute-done.5.refs_1_ = bf16[64,1024]{1,0:T(8,128)(2,1)S(1)} collective-permute-done((bf16[64,1024]{1,0:T(8,128)(2,1)S(1)}, bf16[64,1024]{1,0:T(8,128)(2,1)S(1)}, u32[]{:S(2)}, u32[]{:S(2)}) %collective-permute-start.5) | collective-permute-done | bytes 131104 | tf_op jit(solution)/shard_map/ppermute | solution.py:258
  31.8 0.7 %finish_high.1 = bf16[32,2,2048]{2,1,0:T(2,128)(2,1)} custom-call(f32[64,1024]{1,0:T(8,128)S(1)} %own.1.refs_0_, bf16[64,1024]{1,0:T(8,128)(2,1)S(1)} %collective-permute-done.5.refs_1_, bf16[32,2,2048]{2,1,0:T(2,128)(2,1)} %finish_low.1.refs_2_), custom_call_target="tpu_custom_call", output_to_operand_aliasing={{}: (2, {})} | custom-call | tf_op jit(solution)/shard_map/finish_high/pallas_call | solution.py:434
  (1 shorter events, 0.0 us)
Async XLA Ops:
  0.0 9.5 %collective-permute-start = (bf16[32,2,2048]{2,1,0:T(2,128)(2,1)}, bf16[32,2,2048]{2,1,0:T(2,128)(2,1)S(1)}, u32[]{:S(2)}, u32[]{:S(2)}) collective-permute-start(bf16[32,2,2048]{2,1,0:T(2,128)(2,1)} %probes.1), channel_id=1, source_target_pairs={{0,2},{2,0},{1,3},{3,1},{4,6},{6,4},{5,7},{7,5},{8,10},{10,8},{9,1... | collective-permute-start | bytes 786440 | tf_op jit(solution)/shard_map/ppermute | solution.py:258
  11.1 5.6 %collective-permute-start.3 = (bf16[272,128]{1,0:T(8,128)(2,1)S(1)}, bf16[272,128]{1,0:T(8,128)(2,1)S(1)}, u32[]{:S(2)}, u32[]{:S(2)}) collective-permute-start(bf16[272,128]{1,0:T(8,128)(2,1)S(1)} %get-tuple-element.33), channel_id=1, source_target_pairs={{0,6},{2,4},{4,2},{6,0},{8,14},{10,12},{12,10},{14,8},{1,7},{3,5},... | collective-permute-start | bytes 208904 | tf_op jit(solution)/shard_map/ppermute | solution.py:271
  14.0 4.3 %collective-permute-start.2 = (bf16[272,128]{1,0:T(8,128)(2,1)S(1)}, bf16[272,128]{1,0:T(8,128)(2,1)S(1)}, u32[]{:S(2)}, u32[]{:S(2)}) collective-permute-start(bf16[272,128]{1,0:T(8,128)(2,1)S(1)} %get-tuple-element.33), channel_id=1, source_target_pairs={{0,4},{2,6},{4,0},{6,2},{8,12},{10,14},{12,8},{14,10},{1,5},{3,7},... | collective-permute-start | bytes 208904 | tf_op jit(solution)/shard_map/ppermute | solution.py:271
  14.4 4.3 %collective-permute-start.1 = (bf16[272,128]{1,0:T(8,128)(2,1)S(1)}, bf16[272,128]{1,0:T(8,128)(2,1)S(1)}, u32[]{:S(2)}, u32[]{:S(2)}) collective-permute-start(bf16[272,128]{1,0:T(8,128)(2,1)S(1)} %get-tuple-element.33), channel_id=1, source_target_pairs={{0,2},{2,0},{4,6},{6,4},{8,10},{10,8},{12,14},{14,12},{1,3},{3,1},... | collective-permute-start | bytes 208904 | tf_op jit(solution)/shard_map/ppermute | solution.py:271
  18.7 5.3 %collective-permute-start.4 = (bf16[272,128]{1,0:T(8,128)(2,1)S(1)}, bf16[272,128]{1,0:T(8,128)(2,1)S(1)}, u32[]{:S(2)}, u32[]{:S(2)}) collective-permute-start(bf16[272,128]{1,0:T(8,128)(2,1)S(1)} %get-tuple-element.43), channel_id=1, source_target_pairs={{0,8},{2,10},{4,12},{6,14},{8,0},{10,2},{12,4},{14,6},{1,9},{3,11}... | collective-permute-start | bytes 208904 | tf_op jit(solution)/shard_map/ppermute | solution.py:271
  25.3 5.0 %collective-permute-start.6 = (bf16[64,1024]{1,0:T(8,128)(2,1)S(1)}, bf16[64,1024]{1,0:T(8,128)(2,1)S(1)}, u32[]{:S(2)}, u32[]{:S(2)}) collective-permute-start(bf16[64,1024]{1,0:T(8,128)(2,1)S(1)} %get-tuple-element.41.refs_0_), channel_id=1, source_target_pairs={{0,2},{2,0},{1,3},{3,1},{4,6},{6,4},{5,7},{7,5},{8,10},{10,8},{9,1... | collective-permute-start | bytes 393224 | tf_op jit(solution)/shard_map/ppermute | solution.py:258
  26.4 5.4 %collective-permute-start.5 = (bf16[64,1024]{1,0:T(8,128)(2,1)S(1)}, bf16[64,1024]{1,0:T(8,128)(2,1)S(1)}, u32[]{:S(2)}, u32[]{:S(2)}) collective-permute-start(bf16[64,1024]{1,0:T(8,128)(2,1)S(1)} %get-tuple-element.40), channel_id=1, source_target_pairs={{0,2},{2,0},{1,3},{3,1},{4,6},{6,4},{5,7},{7,5},{8,10},{10,8},{9,1... | collective-permute-start | bytes 393224 | tf_op jit(solution)/shard_map/ppermute | solution.py:258

commit v5 on v4

--- a/solution.py
+++ b/solution.py
@@ -197,16 +197,18 @@
     near, far, table, row_factor, wide_b, held, place, step_of,
     back, adjoint, weights, total,
 ):
-    total[...] = near[...] + far[...].astype(F32)
     block_rows = table.shape[1]
     slots = place.shape[0]
     lane = lax.broadcasted_iota(jnp.int32, (1, block_rows), 1).astype(F32)
+    signs = slice(blocks * count, blocks * (count + 2))
+    total[...] = near[signs, :] + far[signs, :].astype(F32)
     for e in range(slots):
         target = place[e]
-        live = total[pl.ds(blocks * count + target, 1), :]
-        error = total[pl.ds(blocks * count + blocks + target, 1), :]
+        live = total[pl.ds(target, 1), :]
+        error = total[pl.ds(blocks + target, 1), :]
         mask = jnp.where(lane < live, 1.0, 0.0)
-        residual = total[pl.ds(pl.multiple_of(target * count, count), count), :] * mask
+        at = pl.ds(pl.multiple_of(target * count, count), count)
+        residual = (near[at, :] + far[at, :].astype(F32)) * mask
         precision = table[0]
         for n in range(1, table.shape[0]):
             precision = jnp.where(error == n, table[n], precision)
@@ -396,7 +398,7 @@
         out_specs=[in_vmem] * 2,
         scratch_shapes=[
             pltpu.VMEM((size, slots * block_rows), BF16),
-            pltpu.VMEM(base.shape, F32),
+            pltpu.VMEM((2 * blocks, block_rows), F32),
         ],
         compiler_params=params,
         name="adjoint",

time: 32.7 us -> 32.6 us (level)
  no operation moved by 1% of the time
where the time goes in v5:
time: 32.6 us; the launch traced here: 32.5 us
  starting transfers between devices  11.3 us (35%)
  waiting for transfers between devices  10.4 us (32%)
  Pallas kernels  8.7 us (27%)
  between operations  2 us (6%)
    ppermute x4, waiting for transfers between devices, hop(): lax.ppermute(value, ('tile', 'tm'), [(i, i ^ flip) for i in range(tiles *...  6.62 us
    ppermute x4, starting transfers between devices, hop(): lax.ppermute(value, ('tile', 'tm'), [(i, i ^ flip) for i in range(tiles *...  6.21 us
    ppermute x3, starting transfers between devices, exchange(): return lax.ppermute(value, axis, [(i, i ^ distance) for i in range(size)])  5.09 us
    ppermute x3, waiting for transfers between devices, exchange(): return lax.ppermute(value, axis, [(i, i ^ distance) for i in range(size)])  3.74 us
    pallas_call x1, Pallas kernels, per_device(): pl.pallas_call(functools.partial(prepare_kernel, groups, steps, count, bl...  3.2 us
    pallas_call x1, Pallas kernels, per_device(): pl.pallas_call(functools.partial(predict_kernel, groups, steps, count), o...  1.67 us
    pallas_call x1, Pallas kernels, per_device(): pl.pallas_call(functools.partial(adjoint_kernel, steps, count, blocks), o...  1.32 us
    pallas_call x1, Pallas kernels, per_device(): pl.pallas_call(functools.partial(finish_low_kernel, groups, low_lanes), o...  0.93 us
  transfers between devices with their start and end apart: 7, of which 7 were waited for; matrix products, arithmetic and copies ran while one was open for 0% of the time, Pallas kernels for 15%

profile of v5, /device:TPU:0, one launch (start us, length us, event | category | flops | bytes accessed | tf_op | source)
XLA Modules:
  0.0 32.5 jit_solution(5007905382814261353)
XLA Ops:
  0.0 2.9 %collective-permute-start = (bf16[32,2,2048]{2,1,0:T(2,128)(2,1)}, bf16[32,2,2048]{2,1,0:T(2,128)(2,1)S(1)}, u32[]{:S(2)}, u32[]{:S(2)}) collective-permute-start(bf16[32,2,2048]{2,1,0:T(2,128)(2,1)} %probes.1), channel_id=1, source_target_pairs={{0,2},{2,0},{1,3},{3,1},{4,6},{6,4},{5,7},{7,5},{8,10},{10,8},{9,1... | collective-permute-start | bytes 786440 | tf_op jit(solution)/shard_map/ppermute | solution.py:260
  4.9 0.1 pad_add_fusion.counts
  5.0 3.2 %prepare.1 = (bf16[1024,2048]{1,0:T(8,128)(2,1)S(1)}, bf16[2048,1024]{1,0:T(8,128)(2,1)S(1)}, bf16[32,2,2048]{2,1,0:T(2,128)(2,1)S(1)}, f32[4,128,128]{2,1,0:T(8...) custom-call(bf16[1024,2048]{1,0:T(8,128)(2,1)} %bitcast.2, ...), custom_call_target="tpu_custom_call" | custom-call | tf_op jit(solution)/shard_map/prepare/pallas_call | solution.py:328
  8.2 1.3 %collective-permute-done.refs_1_ = bf16[32,2,2048]{2,1,0:T(2,128)(2,1)S(1)} collective-permute-done((bf16[32,2,2048]{2,1,0:T(2,128)(2,1)}, bf16[32,2,2048]{2,1,0:T(2,128)(2,1)S(1)}, u32[]{:S(2)}, u32[]{:S(2)}) %collective-permute-start) | collective-permute-done | bytes 262176 | tf_op jit(solution)/shard_map/ppermute | solution.py:260
  9.5 1.7 %predict.1 = (f32[272,128]{1,0:T(8,128)S(1)}, bf16[272,128]{1,0:T(8,128)(2,1)S(1)}) custom-call(bf16[32,2,2048]{2,1,0:T(2,128)(2,1)S(1)} %get-tuple-element.24.refs_0_.probes.refs_2_, bf16[32,2,2048]{2,1,0:T(2,128)(2,1)S(1)} %collective-permute-done.refs_1_, bf16[128,128]{1,0:T(8,128)(2,1)S(1)} %get-tuple-element.25.refs_2_, ...), custom_call_target="tpu_custom_call" | custom-call | tf_op jit(solution)/shard_map/predict/pallas_call | solution.py:373
  11.1 2.8 %collective-permute-start.3 = (bf16[272,128]{1,0:T(8,128)(2,1)S(1)}, bf16[272,128]{1,0:T(8,128)(2,1)S(1)}, u32[]{:S(2)}, u32[]{:S(2)}) collective-permute-start(bf16[272,128]{1,0:T(8,128)(2,1)S(1)} %get-tuple-element.33), channel_id=1, source_target_pairs={{0,6},{2,4},{4,2},{6,0},{8,14},{10,12},{12,10},{14,8},{1,7},{3,5},... | collective-permute-start | bytes 208904 | tf_op jit(solution)/shard_map/ppermute | solution.py:273
  14.0 0.4 %collective-permute-start.2 = (bf16[272,128]{1,0:T(8,128)(2,1)S(1)}, bf16[272,128]{1,0:T(8,128)(2,1)S(1)}, u32[]{:S(2)}, u32[]{:S(2)}) collective-permute-start(bf16[272,128]{1,0:T(8,128)(2,1)S(1)} %get-tuple-element.33), channel_id=1, source_target_pairs={{0,4},{2,6},{4,0},{6,2},{8,12},{10,14},{12,8},{14,10},{1,5},{3,7},... | collective-permute-start | bytes 208904 | tf_op jit(solution)/shard_map/ppermute | solution.py:273
  14.4 0.3 collective-permute-start.1
  14.7 2.0 %collective-permute-done.3 = bf16[272,128]{1,0:T(8,128)(2,1)S(1)} collective-permute-done((bf16[272,128]{1,0:T(8,128)(2,1)S(1)}, bf16[272,128]{1,0:T(8,128)(2,1)S(1)}, u32[]{:S(2)}, u32[]{:S(2)}) %collective-permute-start.3) | collective-permute-done | bytes 69664 | tf_op jit(solution)/shard_map/ppermute | solution.py:273
  16.7 1.5 %collective-permute-done.2 = bf16[272,128]{1,0:T(8,128)(2,1)S(1)} collective-permute-done((bf16[272,128]{1,0:T(8,128)(2,1)S(1)}, bf16[272,128]{1,0:T(8,128)(2,1)S(1)}, u32[]{:S(2)}, u32[]{:S(2)}) %collective-permute-start.2) | collective-permute-done | bytes 69664 | tf_op jit(solution)/shard_map/ppermute | solution.py:273
  18.3 0.4 %collective-permute-done.1 = bf16[272,128]{1,0:T(8,128)(2,1)S(1)} collective-permute-done((bf16[272,128]{1,0:T(8,128)(2,1)S(1)}, bf16[272,128]{1,0:T(8,128)(2,1)S(1)}, u32[]{:S(2)}, u32[]{:S(2)}) %collective-permute-start.1) | collective-permute-done | bytes 69664 | tf_op jit(solution)/shard_map/ppermute | solution.py:273
  18.7 2.7 %collective-permute-start.4 = (bf16[272,128]{1,0:T(8,128)(2,1)S(1)}, bf16[272,128]{1,0:T(8,128)(2,1)S(1)}, u32[]{:S(2)}, u32[]{:S(2)}) collective-permute-start(bf16[272,128]{1,0:T(8,128)(2,1)S(1)} %get-tuple-element.43), channel_id=1, source_target_pairs={{0,8},{2,10},{4,12},{6,14},{8,0},{10,2},{12,4},{14,6},{1,9},{3,11}... | collective-permute-start | bytes 208904 | tf_op jit(solution)/shard_map/ppermute | solution.py:273
  21.4 2.6 %collective-permute-done.4.far = bf16[272,128]{1,0:T(8,128)(2,1)S(1)} collective-permute-done((bf16[272,128]{1,0:T(8,128)(2,1)S(1)}, bf16[272,128]{1,0:T(8,128)(2,1)S(1)}, u32[]{:S(2)}, u32[]{:S(2)}) %collective-permute-start.4) | collective-permute-done | bytes 69664 | tf_op jit(solution)/shard_map/ppermute | solution.py:273
  24.0 1.3 %adjoint.1 = (bf16[64,1024]{1,0:T(8,128)(2,1)S(1)}, f32[64,2048]{1,0:T(8,128)S(1)}) custom-call(f32[272,128]{1,0:T(8,128)S(1)} %get-tuple-element.44.near, bf16[272,128]{1,0:T(8,128)(2,1)S(1)} %collective-permute-done.4.far, f32[4,128,128]{2,1,0:T(8,128)S(1)} %get-tuple-element.34.table, f32[16,16]{1,0:T(8,128)S(4)} %get-tuple-element.26.refs_3_.row_factor, ...), custom_call_target="tpu_custom_call" | custom-call | tf_op jit(solution)/shard_map/adjoint/pallas_call | solution.py:391
  25.3 0.4 %collective-permute-start.6 = (bf16[64,1024]{1,0:T(8,128)(2,1)S(1)}, bf16[64,1024]{1,0:T(8,128)(2,1)S(1)}, u32[]{:S(2)}, u32[]{:S(2)}) collective-permute-start(bf16[64,1024]{1,0:T(8,128)(2,1)S(1)} %get-tuple-element.41.refs_0_), channel_id=1, source_target_pairs={{0,2},{2,0},{1,3},{3,1},{4,6},{6,4},{5,7},{7,5},{8,10},{10,8},{9,1... | collective-permute-start | bytes 393224 | tf_op jit(solution)/shard_map/ppermute | solution.py:260
  25.7 0.6 %adjoint_rest.1 = (bf16[64,1024]{1,0:T(8,128)(2,1)S(1)}, bf16[128,1024]{1,0:T(8,128)(2,1)S(1)}) custom-call(f32[64,2048]{1,0:T(8,128)S(1)} %get-tuple-element.37.adjoint, f32[16,16]{1,0:T(8,128)S(4)} %get-tuple-element.26.refs_3_.row_factor, bf16[256,256]{1,0:T(8,128)(2,1)S(1)} %get-tuple-element.35.wide_b, bf16[2,128,128]{2,1,0:T(8,128)(2,1)S(1)} %get-tuple-element.38.unmix_b), custom_call_target="tpu_custom_call" | custom-call | tf_op jit(solution)/shard_map/adjoint_rest/pallas_call | solution.py:407
  26.4 1.8 %collective-permute-start.5 = (bf16[64,1024]{1,0:T(8,128)(2,1)S(1)}, bf16[64,1024]{1,0:T(8,128)(2,1)S(1)}, u32[]{:S(2)}, u32[]{:S(2)}) collective-permute-start(bf16[64,1024]{1,0:T(8,128)(2,1)S(1)} %get-tuple-element.40), channel_id=1, source_target_pairs={{0,2},{2,0},{1,3},{3,1},{4,6},{6,4},{5,7},{7,5},{8,10},{10,8},{9,1... | collective-permute-start | bytes 393224 | tf_op jit(solution)/shard_map/ppermute | solution.py:260
  28.1 0.2 own.1.refs_0_
  28.4 2.0 %collective-permute-done.6.refs_1_ = bf16[64,1024]{1,0:T(8,128)(2,1)S(1)} collective-permute-done((bf16[64,1024]{1,0:T(8,128)(2,1)S(1)}, bf16[64,1024]{1,0:T(8,128)(2,1)S(1)}, u32[]{:S(2)}, u32[]{:S(2)}) %collective-permute-start.6) | collective-permute-done | bytes 131104 | tf_op jit(solution)/shard_map/ppermute | solution.py:260
  30.4 0.9 %finish_low.1.refs_2_ = bf16[32,2,2048]{2,1,0:T(2,128)(2,1)} custom-call(bf16[64,1024]{1,0:T(8,128)(2,1)S(1)} %get-tuple-element.41.refs_0_, bf16[64,1024]{1,0:T(8,128)(2,1)S(1)} %collective-permute-done.6.refs_1_, bf16[32,2,2048]{2,1,0:T(2,128)(2,1)S(1)} %get-tuple-element.24.refs_0_.probes.refs_2_, bf16[128,128]{1,0:T(8,128)(2,1)S(1)} %get-tuple-element.42.refs_3_), custom_call_target="tpu_custom_call" | custom-call | tf_op jit(solution)/shard_map/finish_low/pallas_call | solution.py:427
  31.3 0.5 %collective-permute-done.5.refs_1_ = bf16[64,1024]{1,0:T(8,128)(2,1)S(1)} collective-permute-done((bf16[64,1024]{1,0:T(8,128)(2,1)S(1)}, bf16[64,1024]{1,0:T(8,128)(2,1)S(1)}, u32[]{:S(2)}, u32[]{:S(2)}) %collective-permute-start.5) | collective-permute-done | bytes 131104 | tf_op jit(solution)/shard_map/ppermute | solution.py:260
  31.8 0.7 %finish_high.1 = bf16[32,2,2048]{2,1,0:T(2,128)(2,1)} custom-call(f32[64,1024]{1,0:T(8,128)S(1)} %own.1.refs_0_, bf16[64,1024]{1,0:T(8,128)(2,1)S(1)} %collective-permute-done.5.refs_1_, bf16[32,2,2048]{2,1,0:T(2,128)(2,1)} %finish_low.1.refs_2_), custom_call_target="tpu_custom_call", output_to_operand_aliasing={{}: (2, {})} | custom-call | tf_op jit(solution)/shard_map/finish_high/pallas_call | solution.py:436
  (1 shorter events, 0.0 us)
Async XLA Ops:
  0.0 9.5 %collective-permute-start = (bf16[32,2,2048]{2,1,0:T(2,128)(2,1)}, bf16[32,2,2048]{2,1,0:T(2,128)(2,1)S(1)}, u32[]{:S(2)}, u32[]{:S(2)}) collective-permute-start(bf16[32,2,2048]{2,1,0:T(2,128)(2,1)} %probes.1), channel_id=1, source_target_pairs={{0,2},{2,0},{1,3},{3,1},{4,6},{6,4},{5,7},{7,5},{8,10},{10,8},{9,1... | collective-permute-start | bytes 786440 | tf_op jit(solution)/shard_map/ppermute | solution.py:260
  11.1 5.6 %collective-permute-start.3 = (bf16[272,128]{1,0:T(8,128)(2,1)S(1)}, bf16[272,128]{1,0:T(8,128)(2,1)S(1)}, u32[]{:S(2)}, u32[]{:S(2)}) collective-permute-start(bf16[272,128]{1,0:T(8,128)(2,1)S(1)} %get-tuple-element.33), channel_id=1, source_target_pairs={{0,6},{2,4},{4,2},{6,0},{8,14},{10,12},{12,10},{14,8},{1,7},{3,5},... | collective-permute-start | bytes 208904 | tf_op jit(solution)/shard_map/ppermute | solution.py:273
  14.0 4.3 %collective-permute-start.2 = (bf16[272,128]{1,0:T(8,128)(2,1)S(1)}, bf16[272,128]{1,0:T(8,128)(2,1)S(1)}, u32[]{:S(2)}, u32[]{:S(2)}) collective-permute-start(bf16[272,128]{1,0:T(8,128)(2,1)S(1)} %get-tuple-element.33), channel_id=1, source_target_pairs={{0,4},{2,6},{4,0},{6,2},{8,12},{10,14},{12,8},{14,10},{1,5},{3,7},... | collective-permute-start | bytes 208904 | tf_op jit(solution)/shard_map/ppermute | solution.py:273
  14.4 4.3 %collective-permute-start.1 = (bf16[272,128]{1,0:T(8,128)(2,1)S(1)}, bf16[272,128]{1,0:T(8,128)(2,1)S(1)}, u32[]{:S(2)}, u32[]{:S(2)}) collective-permute-start(bf16[272,128]{1,0:T(8,128)(2,1)S(1)} %get-tuple-element.33), channel_id=1, source_target_pairs={{0,2},{2,0},{4,6},{6,4},{8,10},{10,8},{12,14},{14,12},{1,3},{3,1},... | collective-permute-start | bytes 208904 | tf_op jit(solution)/shard_map/ppermute | solution.py:273
  18.7 5.3 %collective-permute-start.4 = (bf16[272,128]{1,0:T(8,128)(2,1)S(1)}, bf16[272,128]{1,0:T(8,128)(2,1)S(1)}, u32[]{:S(2)}, u32[]{:S(2)}) collective-permute-start(bf16[272,128]{1,0:T(8,128)(2,1)S(1)} %get-tuple-element.43), channel_id=1, source_target_pairs={{0,8},{2,10},{4,12},{6,14},{8,0},{10,2},{12,4},{14,6},{1,9},{3,11}... | collective-permute-start | bytes 208904 | tf_op jit(solution)/shard_map/ppermute | solution.py:273
  25.3 5.0 %collective-permute-start.6 = (bf16[64,1024]{1,0:T(8,128)(2,1)S(1)}, bf16[64,1024]{1,0:T(8,128)(2,1)S(1)}, u32[]{:S(2)}, u32[]{:S(2)}) collective-permute-start(bf16[64,1024]{1,0:T(8,128)(2,1)S(1)} %get-tuple-element.41.refs_0_), channel_id=1, source_target_pairs={{0,2},{2,0},{1,3},{3,1},{4,6},{6,4},{5,7},{7,5},{8,10},{10,8},{9,1... | collective-permute-start | bytes 393224 | tf_op jit(solution)/shard_map/ppermute | solution.py:260
  26.4 5.4 %collective-permute-start.5 = (bf16[64,1024]{1,0:T(8,128)(2,1)S(1)}, bf16[64,1024]{1,0:T(8,128)(2,1)S(1)}, u32[]{:S(2)}, u32[]{:S(2)}) collective-permute-start(bf16[64,1024]{1,0:T(8,128)(2,1)S(1)} %get-tuple-element.40), channel_id=1, source_target_pairs={{0,2},{2,0},{1,3},{3,1},{4,6},{6,4},{5,7},{7,5},{8,10},{10,8},{9,1... | collective-permute-start | bytes 393224 | tf_op jit(solution)/shard_map/ppermute | solution.py:260

commit v6 on v4

--- a/solution.py
+++ b/solution.py
@@ -223,12 +223,12 @@
     *sent, stacked = refs
     row_mix(adjoint, row_factor, True, wide_b[...], stacked, first)
     for n, z in enumerate(sent):
-        z[...] = unmix(unmix_b[n + 1], stacked[...]).astype(BF16)
+        z[...] = unmix(unmix_b[n + 1][:, : stacked.shape[0]], stacked[...]).astype(BF16)
 
 
 def own_kernel(lanes, probes, stacked, unmix_b, out):
     before = probes[:, :, lanes].reshape(out.shape).astype(F32)
-    out[...] = before + unmix(unmix_b[0], stacked[...])
+    out[...] = before + unmix(unmix_b[0][:, : stacked.shape[0]], stacked[...])
 
 
 def put(value, made, out, lanes, sem):
@@ -405,7 +405,7 @@
     *sent, stacked = pl.pallas_call(
         functools.partial(adjoint_rest_kernel, half // LANES),
         out_shape=[jax.ShapeDtypeStruct((size, half), BF16)] * (groups - 1)
-        + [jax.ShapeDtypeStruct((2 * size, half), BF16)],
+        + [jax.ShapeDtypeStruct((size, half), BF16)],
         in_specs=[in_vmem, in_smem, in_vmem, in_vmem],
         out_specs=[in_vmem] * groups,
         compiler_params=params,

time: 32.7 us -> 32.7 us (level)
  no operation moved by 1% of the time
where the time goes in v6:
time: 32.7 us; the launch traced here: 32.5 us
  starting transfers between devices  11.3 us (35%)
  waiting for transfers between devices  10.4 us (32%)
  Pallas kernels  8.69 us (27%)
  between operations  2 us (6%)
    ppermute x4, waiting for transfers between devices, hop(): lax.ppermute(value, ('tile', 'tm'), [(i, i ^ flip) for i in range(tiles *...  6.64 us
    ppermute x4, starting transfers between devices, hop(): lax.ppermute(value, ('tile', 'tm'), [(i, i ^ flip) for i in range(tiles *...  6.21 us
    ppermute x3, starting transfers between devices, exchange(): return lax.ppermute(value, axis, [(i, i ^ distance) for i in range(size)])  5.1 us
    ppermute x3, waiting for transfers between devices, exchange(): return lax.ppermute(value, axis, [(i, i ^ distance) for i in range(size)])  3.75 us
    pallas_call x1, Pallas kernels, per_device(): pl.pallas_call(functools.partial(prepare_kernel, groups, steps, count, bl...  3.2 us
    pallas_call x1, Pallas kernels, per_device(): pl.pallas_call(functools.partial(predict_kernel, groups, steps, count), o...  1.66 us
    pallas_call x1, Pallas kernels, per_device(): pl.pallas_call(functools.partial(adjoint_kernel, steps, count, blocks), o...  1.33 us
    pallas_call x1, Pallas kernels, per_device(): pl.pallas_call(functools.partial(finish_low_kernel, groups, low_lanes), o...  0.93 us
  transfers between devices with their start and end apart: 7, of which 7 were waited for; matrix products, arithmetic and copies ran while one was open for 0% of the time, Pallas kernels for 15%

profile of v6, /device:TPU:0, one launch (start us, length us, event | category | flops | bytes accessed | tf_op | source)
XLA Modules:
  0.0 32.5 jit_solution(15831757176004011865)
XLA Ops:
  0.0 2.9 %collective-permute-start = (bf16[32,2,2048]{2,1,0:T(2,128)(2,1)}, bf16[32,2,2048]{2,1,0:T(2,128)(2,1)S(1)}, u32[]{:S(2)}, u32[]{:S(2)}) collective-permute-start(bf16[32,2,2048]{2,1,0:T(2,128)(2,1)} %probes.1), channel_id=1, source_target_pairs={{0,2},{2,0},{1,3},{3,1},{4,6},{6,4},{5,7},{7,5},{8,10},{10,8},{9,1... | collective-permute-start | bytes 786440 | tf_op jit(solution)/shard_map/ppermute | solution.py:258
  4.9 0.1 pad_add_fusion.counts
  5.0 3.2 %prepare.1 = (bf16[1024,2048]{1,0:T(8,128)(2,1)S(1)}, bf16[2048,1024]{1,0:T(8,128)(2,1)S(1)}, bf16[32,2,2048]{2,1,0:T(2,128)(2,1)S(1)}, f32[4,128,128]{2,1,0:T(8...) custom-call(bf16[1024,2048]{1,0:T(8,128)(2,1)} %bitcast.2, ...), custom_call_target="tpu_custom_call" | custom-call | tf_op jit(solution)/shard_map/prepare/pallas_call | solution.py:326
  8.2 1.3 %collective-permute-done.refs_1_ = bf16[32,2,2048]{2,1,0:T(2,128)(2,1)S(1)} collective-permute-done((bf16[32,2,2048]{2,1,0:T(2,128)(2,1)}, bf16[32,2,2048]{2,1,0:T(2,128)(2,1)S(1)}, u32[]{:S(2)}, u32[]{:S(2)}) %collective-permute-start) | collective-permute-done | bytes 262176 | tf_op jit(solution)/shard_map/ppermute | solution.py:258
  9.5 1.7 %predict.1 = (f32[272,128]{1,0:T(8,128)S(1)}, bf16[272,128]{1,0:T(8,128)(2,1)S(1)}) custom-call(bf16[32,2,2048]{2,1,0:T(2,128)(2,1)S(1)} %get-tuple-element.24.refs_0_.probes.refs_2_, bf16[32,2,2048]{2,1,0:T(2,128)(2,1)S(1)} %collective-permute-done.refs_1_, bf16[128,128]{1,0:T(8,128)(2,1)S(1)} %get-tuple-element.25.refs_2_, ...), custom_call_target="tpu_custom_call" | custom-call | tf_op jit(solution)/shard_map/predict/pallas_call | solution.py:371
  11.1 2.8 %collective-permute-start.3 = (bf16[272,128]{1,0:T(8,128)(2,1)S(1)}, bf16[272,128]{1,0:T(8,128)(2,1)S(1)}, u32[]{:S(2)}, u32[]{:S(2)}) collective-permute-start(bf16[272,128]{1,0:T(8,128)(2,1)S(1)} %get-tuple-element.33), channel_id=1, source_target_pairs={{0,6},{2,4},{4,2},{6,0},{8,14},{10,12},{12,10},{14,8},{1,7},{3,5},... | collective-permute-start | bytes 208904 | tf_op jit(solution)/shard_map/ppermute | solution.py:271
  14.0 0.4 %collective-permute-start.2 = (bf16[272,128]{1,0:T(8,128)(2,1)S(1)}, bf16[272,128]{1,0:T(8,128)(2,1)S(1)}, u32[]{:S(2)}, u32[]{:S(2)}) collective-permute-start(bf16[272,128]{1,0:T(8,128)(2,1)S(1)} %get-tuple-element.33), channel_id=1, source_target_pairs={{0,4},{2,6},{4,0},{6,2},{8,12},{10,14},{12,8},{14,10},{1,5},{3,7},... | collective-permute-start | bytes 208904 | tf_op jit(solution)/shard_map/ppermute | solution.py:271
  14.4 0.3 collective-permute-start.1
  14.7 2.1 %collective-permute-done.3 = bf16[272,128]{1,0:T(8,128)(2,1)S(1)} collective-permute-done((bf16[272,128]{1,0:T(8,128)(2,1)S(1)}, bf16[272,128]{1,0:T(8,128)(2,1)S(1)}, u32[]{:S(2)}, u32[]{:S(2)}) %collective-permute-start.3) | collective-permute-done | bytes 69664 | tf_op jit(solution)/shard_map/ppermute | solution.py:271
  16.7 1.5 %collective-permute-done.2 = bf16[272,128]{1,0:T(8,128)(2,1)S(1)} collective-permute-done((bf16[272,128]{1,0:T(8,128)(2,1)S(1)}, bf16[272,128]{1,0:T(8,128)(2,1)S(1)}, u32[]{:S(2)}, u32[]{:S(2)}) %collective-permute-start.2) | collective-permute-done | bytes 69664 | tf_op jit(solution)/shard_map/ppermute | solution.py:271
  18.3 0.4 %collective-permute-done.1 = bf16[272,128]{1,0:T(8,128)(2,1)S(1)} collective-permute-done((bf16[272,128]{1,0:T(8,128)(2,1)S(1)}, bf16[272,128]{1,0:T(8,128)(2,1)S(1)}, u32[]{:S(2)}, u32[]{:S(2)}) %collective-permute-start.1) | collective-permute-done | bytes 69664 | tf_op jit(solution)/shard_map/ppermute | solution.py:271
  18.7 2.7 %collective-permute-start.4 = (bf16[272,128]{1,0:T(8,128)(2,1)S(1)}, bf16[272,128]{1,0:T(8,128)(2,1)S(1)}, u32[]{:S(2)}, u32[]{:S(2)}) collective-permute-start(bf16[272,128]{1,0:T(8,128)(2,1)S(1)} %get-tuple-element.43), channel_id=1, source_target_pairs={{0,8},{2,10},{4,12},{6,14},{8,0},{10,2},{12,4},{14,6},{1,9},{3,11}... | collective-permute-start | bytes 208904 | tf_op jit(solution)/shard_map/ppermute | solution.py:271
  21.4 2.6 %collective-permute-done.4.far = bf16[272,128]{1,0:T(8,128)(2,1)S(1)} collective-permute-done((bf16[272,128]{1,0:T(8,128)(2,1)S(1)}, bf16[272,128]{1,0:T(8,128)(2,1)S(1)}, u32[]{:S(2)}, u32[]{:S(2)}) %collective-permute-start.4) | collective-permute-done | bytes 69664 | tf_op jit(solution)/shard_map/ppermute | solution.py:271
  24.0 1.3 %adjoint.1 = (bf16[64,1024]{1,0:T(8,128)(2,1)S(1)}, f32[64,2048]{1,0:T(8,128)S(1)}) custom-call(f32[272,128]{1,0:T(8,128)S(1)} %get-tuple-element.44.near, bf16[272,128]{1,0:T(8,128)(2,1)S(1)} %collective-permute-done.4.far, f32[4,128,128]{2,1,0:T(8,128)S(1)} %get-tuple-element.34.table, f32[16,16]{1,0:T(8,128)S(4)} %get-tuple-element.26.refs_3_.row_factor, ...), custom_call_target="tpu_custom_call" | custom-call | tf_op jit(solution)/shard_map/adjoint/pallas_call | solution.py:389
  25.4 0.3 %collective-permute-start.6 = (bf16[64,1024]{1,0:T(8,128)(2,1)S(1)}, bf16[64,1024]{1,0:T(8,128)(2,1)S(1)}, u32[]{:S(2)}, u32[]{:S(2)}) collective-permute-start(bf16[64,1024]{1,0:T(8,128)(2,1)S(1)} %get-tuple-element.41.refs_0_), channel_id=1, source_target_pairs={{0,2},{2,0},{1,3},{3,1},{4,6},{6,4},{5,7},{7,5},{8,10},{10,8},{9,1... | collective-permute-start | bytes 393224 | tf_op jit(solution)/shard_map/ppermute | solution.py:258
  25.7 0.6 %adjoint_rest.1 = (bf16[64,1024]{1,0:T(8,128)(2,1)S(1)}, bf16[64,1024]{1,0:T(8,128)(2,1)S(1)}) custom-call(f32[64,2048]{1,0:T(8,128)S(1)} %get-tuple-element.37.adjoint, f32[16,16]{1,0:T(8,128)S(4)} %get-tuple-element.26.refs_3_.row_factor, bf16[256,256]{1,0:T(8,128)(2,1)S(1)} %get-tuple-element.35.wide_b, bf16[2,128,128]{2,1,0:T(8,128)(2,1)S(1)} %get-tuple-element.38.unmix_b), custom_call_target="tpu_custom_call" | custom-call | tf_op jit(solution)/shard_map/adjoint_rest/pallas_call | solution.py:405
  26.3 1.8 %collective-permute-start.5 = (bf16[64,1024]{1,0:T(8,128)(2,1)S(1)}, bf16[64,1024]{1,0:T(8,128)(2,1)S(1)}, u32[]{:S(2)}, u32[]{:S(2)}) collective-permute-start(bf16[64,1024]{1,0:T(8,128)(2,1)S(1)} %get-tuple-element.40), channel_id=1, source_target_pairs={{0,2},{2,0},{1,3},{3,1},{4,6},{6,4},{5,7},{7,5},{8,10},{10,8},{9,1... | collective-permute-start | bytes 393224 | tf_op jit(solution)/shard_map/ppermute | solution.py:258
  28.2 0.2 own.1.refs_0_
  28.4 2.0 %collective-permute-done.6.refs_1_ = bf16[64,1024]{1,0:T(8,128)(2,1)S(1)} collective-permute-done((bf16[64,1024]{1,0:T(8,128)(2,1)S(1)}, bf16[64,1024]{1,0:T(8,128)(2,1)S(1)}, u32[]{:S(2)}, u32[]{:S(2)}) %collective-permute-start.6) | collective-permute-done | bytes 131104 | tf_op jit(solution)/shard_map/ppermute | solution.py:258
  30.4 0.9 %finish_low.1.refs_2_ = bf16[32,2,2048]{2,1,0:T(2,128)(2,1)} custom-call(bf16[64,1024]{1,0:T(8,128)(2,1)S(1)} %get-tuple-element.41.refs_0_, bf16[64,1024]{1,0:T(8,128)(2,1)S(1)} %collective-permute-done.6.refs_1_, bf16[32,2,2048]{2,1,0:T(2,128)(2,1)S(1)} %get-tuple-element.24.refs_0_.probes.refs_2_, bf16[128,128]{1,0:T(8,128)(2,1)S(1)} %get-tuple-element.42.refs_3_), custom_call_target="tpu_custom_call" | custom-call | tf_op jit(solution)/shard_map/finish_low/pallas_call | solution.py:425
  31.3 0.5 %collective-permute-done.5.refs_1_ = bf16[64,1024]{1,0:T(8,128)(2,1)S(1)} collective-permute-done((bf16[64,1024]{1,0:T(8,128)(2,1)S(1)}, bf16[64,1024]{1,0:T(8,128)(2,1)S(1)}, u32[]{:S(2)}, u32[]{:S(2)}) %collective-permute-start.5) | collective-permute-done | bytes 131104 | tf_op jit(solution)/shard_map/ppermute | solution.py:258
  31.8 0.7 %finish_high.1 = bf16[32,2,2048]{2,1,0:T(2,128)(2,1)} custom-call(f32[64,1024]{1,0:T(8,128)S(1)} %own.1.refs_0_, bf16[64,1024]{1,0:T(8,128)(2,1)S(1)} %collective-permute-done.5.refs_1_, bf16[32,2,2048]{2,1,0:T(2,128)(2,1)} %finish_low.1.refs_2_), custom_call_target="tpu_custom_call", output_to_operand_aliasing={{}: (2, {})} | custom-call | tf_op jit(solution)/shard_map/finish_high/pallas_call | solution.py:434
  (1 shorter events, 0.0 us)
Async XLA Ops:
  0.0 9.5 %collective-permute-start = (bf16[32,2,2048]{2,1,0:T(2,128)(2,1)}, bf16[32,2,2048]{2,1,0:T(2,128)(2,1)S(1)}, u32[]{:S(2)}, u32[]{:S(2)}) collective-permute-start(bf16[32,2,2048]{2,1,0:T(2,128)(2,1)} %probes.1), channel_id=1, source_target_pairs={{0,2},{2,0},{1,3},{3,1},{4,6},{6,4},{5,7},{7,5},{8,10},{10,8},{9,1... | collective-permute-start | bytes 786440 | tf_op jit(solution)/shard_map/ppermute | solution.py:258
  11.1 5.6 %collective-permute-start.3 = (bf16[272,128]{1,0:T(8,128)(2,1)S(1)}, bf16[272,128]{1,0:T(8,128)(2,1)S(1)}, u32[]{:S(2)}, u32[]{:S(2)}) collective-permute-start(bf16[272,128]{1,0:T(8,128)(2,1)S(1)} %get-tuple-element.33), channel_id=1, source_target_pairs={{0,6},{2,4},{4,2},{6,0},{8,14},{10,12},{12,10},{14,8},{1,7},{3,5},... | collective-permute-start | bytes 208904 | tf_op jit(solution)/shard_map/ppermute | solution.py:271
  14.0 4.3 %collective-permute-start.2 = (bf16[272,128]{1,0:T(8,128)(2,1)S(1)}, bf16[272,128]{1,0:T(8,128)(2,1)S(1)}, u32[]{:S(2)}, u32[]{:S(2)}) collective-permute-start(bf16[272,128]{1,0:T(8,128)(2,1)S(1)} %get-tuple-element.33), channel_id=1, source_target_pairs={{0,4},{2,6},{4,0},{6,2},{8,12},{10,14},{12,8},{14,10},{1,5},{3,7},... | collective-permute-start | bytes 208904 | tf_op jit(solution)/shard_map/ppermute | solution.py:271
  14.4 4.3 %collective-permute-start.1 = (bf16[272,128]{1,0:T(8,128)(2,1)S(1)}, bf16[272,128]{1,0:T(8,128)(2,1)S(1)}, u32[]{:S(2)}, u32[]{:S(2)}) collective-permute-start(bf16[272,128]{1,0:T(8,128)(2,1)S(1)} %get-tuple-element.33), channel_id=1, source_target_pairs={{0,2},{2,0},{4,6},{6,4},{8,10},{10,8},{12,14},{14,12},{1,3},{3,1},... | collective-permute-start | bytes 208904 | tf_op jit(solution)/shard_map/ppermute | solution.py:271
  18.7 5.3 %collective-permute-start.4 = (bf16[272,128]{1,0:T(8,128)(2,1)S(1)}, bf16[272,128]{1,0:T(8,128)(2,1)S(1)}, u32[]{:S(2)}, u32[]{:S(2)}) collective-permute-start(bf16[272,128]{1,0:T(8,128)(2,1)S(1)} %get-tuple-element.43), channel_id=1, source_target_pairs={{0,8},{2,10},{4,12},{6,14},{8,0},{10,2},{12,4},{14,6},{1,9},{3,11}... | collective-permute-start | bytes 208904 | tf_op jit(solution)/shard_map/ppermute | solution.py:271
  25.4 5.0 %collective-permute-start.6 = (bf16[64,1024]{1,0:T(8,128)(2,1)S(1)}, bf16[64,1024]{1,0:T(8,128)(2,1)S(1)}, u32[]{:S(2)}, u32[]{:S(2)}) collective-permute-start(bf16[64,1024]{1,0:T(8,128)(2,1)S(1)} %get-tuple-element.41.refs_0_), channel_id=1, source_target_pairs={{0,2},{2,0},{1,3},{3,1},{4,6},{6,4},{5,7},{7,5},{8,10},{10,8},{9,1... | collective-permute-start | bytes 393224 | tf_op jit(solution)/shard_map/ppermute | solution.py:258
  26.3 5.5 %collective-permute-start.5 = (bf16[64,1024]{1,0:T(8,128)(2,1)S(1)}, bf16[64,1024]{1,0:T(8,128)(2,1)S(1)}, u32[]{:S(2)}, u32[]{:S(2)}) collective-permute-start(bf16[64,1024]{1,0:T(8,128)(2,1)S(1)} %get-tuple-element.40), channel_id=1, source_target_pairs={{0,2},{2,0},{1,3},{3,1},{4,6},{6,4},{5,7},{7,5},{8,10},{10,8},{9,1... | collective-permute-start | bytes 393224 | tf_op jit(solution)/shard_map/ppermute | solution.py:258

commit v7 on v5

--- a/solution.py
+++ b/solution.py
@@ -225,12 +225,12 @@
     *sent, stacked = refs
     row_mix(adjoint, row_factor, True, wide_b[...], stacked, first)
     for n, z in enumerate(sent):
-        z[...] = unmix(unmix_b[n + 1], stacked[...]).astype(BF16)
+        z[...] = unmix(unmix_b[n + 1][:, : stacked.shape[0]], stacked[...]).astype(BF16)
 
 
 def own_kernel(lanes, probes, stacked, unmix_b, out):
     before = probes[:, :, lanes].reshape(out.shape).astype(F32)
-    out[...] = before + unmix(unmix_b[0], stacked[...])
+    out[...] = before + unmix(unmix_b[0][:, : stacked.shape[0]], stacked[...])
 
 
 def put(value, made, out, lanes, sem):
@@ -407,7 +407,7 @@
     *sent, stacked = pl.pallas_call(
         functools.partial(adjoint_rest_kernel, half // LANES),
         out_shape=[jax.ShapeDtypeStruct((size, half), BF16)] * (groups - 1)
-        + [jax.ShapeDtypeStruct((2 * size, half), BF16)],
+        + [jax.ShapeDtypeStruct((size, half), BF16)],
         in_specs=[in_vmem, in_smem, in_vmem, in_vmem],
         out_specs=[in_vmem] * groups,
         compiler_params=params,

time: 32.6 us -> 32.7 us (level)
  no operation moved by 1% of the time
where the time goes in v7:
time: 32.7 us; the launch traced here: 32.5 us
  starting transfers between devices  11.3 us (35%)
  waiting for transfers between devices  10.4 us (32%)
  Pallas kernels  8.68 us (27%)
  between operations  1.99 us (6%)
    ppermute x4, waiting for transfers between devices, hop(): lax.ppermute(value, ('tile', 'tm'), [(i, i ^ flip) for i in range(tiles *...  6.65 us
    ppermute x4, starting transfers between devices, hop(): lax.ppermute(value, ('tile', 'tm'), [(i, i ^ flip) for i in range(tiles *...  6.21 us
    ppermute x3, starting transfers between devices, exchange(): return lax.ppermute(value, axis, [(i, i ^ distance) for i in range(size)])  5.09 us
    ppermute x3, waiting for transfers between devices, exchange(): return lax.ppermute(value, axis, [(i, i ^ distance) for i in range(size)])  3.76 us
    pallas_call x1, Pallas kernels, per_device(): pl.pallas_call(functools.partial(prepare_kernel, groups, steps, count, bl...  3.2 us
    pallas_call x1, Pallas kernels, per_device(): pl.pallas_call(functools.partial(predict_kernel, groups, steps, count), o...  1.67 us
    pallas_call x1, Pallas kernels, per_device(): pl.pallas_call(functools.partial(adjoint_kernel, steps, count, blocks), o...  1.33 us
    pallas_call x1, Pallas kernels, per_device(): pl.pallas_call(functools.partial(finish_low_kernel, groups, low_lanes), o...  0.93 us
  transfers between devices with their start and end apart: 7, of which 7 were waited for; matrix products, arithmetic and copies ran while one was open for 0% of the time, Pallas kernels for 15%

profile of v7, /device:TPU:0, one launch (start us, length us, event | category | flops | bytes accessed | tf_op | source)
XLA Modules:
  0.0 32.5 jit_solution(9633306613031018112)
XLA Ops:
  0.0 2.9 %collective-permute-start = (bf16[32,2,2048]{2,1,0:T(2,128)(2,1)}, bf16[32,2,2048]{2,1,0:T(2,128)(2,1)S(1)}, u32[]{:S(2)}, u32[]{:S(2)}) collective-permute-start(bf16[32,2,2048]{2,1,0:T(2,128)(2,1)} %probes.1), channel_id=1, source_target_pairs={{0,2},{2,0},{1,3},{3,1},{4,6},{6,4},{5,7},{7,5},{8,10},{10,8},{9,1... | collective-permute-start | bytes 786440 | tf_op jit(solution)/shard_map/ppermute | solution.py:260
  4.9 0.1 pad_add_fusion.counts
  5.0 3.2 %prepare.1 = (bf16[1024,2048]{1,0:T(8,128)(2,1)S(1)}, bf16[2048,1024]{1,0:T(8,128)(2,1)S(1)}, bf16[32,2,2048]{2,1,0:T(2,128)(2,1)S(1)}, f32[4,128,128]{2,1,0:T(8...) custom-call(bf16[1024,2048]{1,0:T(8,128)(2,1)} %bitcast.2, ...), custom_call_target="tpu_custom_call" | custom-call | tf_op jit(solution)/shard_map/prepare/pallas_call | solution.py:328
  8.2 1.3 %collective-permute-done.refs_1_ = bf16[32,2,2048]{2,1,0:T(2,128)(2,1)S(1)} collective-permute-done((bf16[32,2,2048]{2,1,0:T(2,128)(2,1)}, bf16[32,2,2048]{2,1,0:T(2,128)(2,1)S(1)}, u32[]{:S(2)}, u32[]{:S(2)}) %collective-permute-start) | collective-permute-done | bytes 262176 | tf_op jit(solution)/shard_map/ppermute | solution.py:260
  9.5 1.7 %predict.1 = (f32[272,128]{1,0:T(8,128)S(1)}, bf16[272,128]{1,0:T(8,128)(2,1)S(1)}) custom-call(bf16[32,2,2048]{2,1,0:T(2,128)(2,1)S(1)} %get-tuple-element.24.refs_0_.probes.refs_2_, bf16[32,2,2048]{2,1,0:T(2,128)(2,1)S(1)} %collective-permute-done.refs_1_, bf16[128,128]{1,0:T(8,128)(2,1)S(1)} %get-tuple-element.25.refs_2_, ...), custom_call_target="tpu_custom_call" | custom-call | tf_op jit(solution)/shard_map/predict/pallas_call | solution.py:373
  11.1 2.8 %collective-permute-start.3 = (bf16[272,128]{1,0:T(8,128)(2,1)S(1)}, bf16[272,128]{1,0:T(8,128)(2,1)S(1)}, u32[]{:S(2)}, u32[]{:S(2)}) collective-permute-start(bf16[272,128]{1,0:T(8,128)(2,1)S(1)} %get-tuple-element.33), channel_id=1, source_target_pairs={{0,6},{2,4},{4,2},{6,0},{8,14},{10,12},{12,10},{14,8},{1,7},{3,5},... | collective-permute-start | bytes 208904 | tf_op jit(solution)/shard_map/ppermute | solution.py:273
  14.0 0.4 %collective-permute-start.2 = (bf16[272,128]{1,0:T(8,128)(2,1)S(1)}, bf16[272,128]{1,0:T(8,128)(2,1)S(1)}, u32[]{:S(2)}, u32[]{:S(2)}) collective-permute-start(bf16[272,128]{1,0:T(8,128)(2,1)S(1)} %get-tuple-element.33), channel_id=1, source_target_pairs={{0,4},{2,6},{4,0},{6,2},{8,12},{10,14},{12,8},{14,10},{1,5},{3,7},... | collective-permute-start | bytes 208904 | tf_op jit(solution)/shard_map/ppermute | solution.py:273
  14.4 0.3 collective-permute-start.1
  14.7 2.1 %collective-permute-done.3 = bf16[272,128]{1,0:T(8,128)(2,1)S(1)} collective-permute-done((bf16[272,128]{1,0:T(8,128)(2,1)S(1)}, bf16[272,128]{1,0:T(8,128)(2,1)S(1)}, u32[]{:S(2)}, u32[]{:S(2)}) %collective-permute-start.3) | collective-permute-done | bytes 69664 | tf_op jit(solution)/shard_map/ppermute | solution.py:273
  16.7 1.5 %collective-permute-done.2 = bf16[272,128]{1,0:T(8,128)(2,1)S(1)} collective-permute-done((bf16[272,128]{1,0:T(8,128)(2,1)S(1)}, bf16[272,128]{1,0:T(8,128)(2,1)S(1)}, u32[]{:S(2)}, u32[]{:S(2)}) %collective-permute-start.2) | collective-permute-done | bytes 69664 | tf_op jit(solution)/shard_map/ppermute | solution.py:273
  18.3 0.4 %collective-permute-done.1 = bf16[272,128]{1,0:T(8,128)(2,1)S(1)} collective-permute-done((bf16[272,128]{1,0:T(8,128)(2,1)S(1)}, bf16[272,128]{1,0:T(8,128)(2,1)S(1)}, u32[]{:S(2)}, u32[]{:S(2)}) %collective-permute-start.1) | collective-permute-done | bytes 69664 | tf_op jit(solution)/shard_map/ppermute | solution.py:273
  18.8 2.7 %collective-permute-start.4 = (bf16[272,128]{1,0:T(8,128)(2,1)S(1)}, bf16[272,128]{1,0:T(8,128)(2,1)S(1)}, u32[]{:S(2)}, u32[]{:S(2)}) collective-permute-start(bf16[272,128]{1,0:T(8,128)(2,1)S(1)} %get-tuple-element.43), channel_id=1, source_target_pairs={{0,8},{2,10},{4,12},{6,14},{8,0},{10,2},{12,4},{14,6},{1,9},{3,11}... | collective-permute-start | bytes 208904 | tf_op jit(solution)/shard_map/ppermute | solution.py:273
  21.4 2.6 %collective-permute-done.4.far = bf16[272,128]{1,0:T(8,128)(2,1)S(1)} collective-permute-done((bf16[272,128]{1,0:T(8,128)(2,1)S(1)}, bf16[272,128]{1,0:T(8,128)(2,1)S(1)}, u32[]{:S(2)}, u32[]{:S(2)}) %collective-permute-start.4) | collective-permute-done | bytes 69664 | tf_op jit(solution)/shard_map/ppermute | solution.py:273
  24.0 1.3 %adjoint.1 = (bf16[64,1024]{1,0:T(8,128)(2,1)S(1)}, f32[64,2048]{1,0:T(8,128)S(1)}) custom-call(f32[272,128]{1,0:T(8,128)S(1)} %get-tuple-element.44.near, bf16[272,128]{1,0:T(8,128)(2,1)S(1)} %collective-permute-done.4.far, f32[4,128,128]{2,1,0:T(8,128)S(1)} %get-tuple-element.34.table, f32[16,16]{1,0:T(8,128)S(4)} %get-tuple-element.26.refs_3_.row_factor, ...), custom_call_target="tpu_custom_call" | custom-call | tf_op jit(solution)/shard_map/adjoint/pallas_call | solution.py:391
  25.4 0.3 %collective-permute-start.6 = (bf16[64,1024]{1,0:T(8,128)(2,1)S(1)}, bf16[64,1024]{1,0:T(8,128)(2,1)S(1)}, u32[]{:S(2)}, u32[]{:S(2)}) collective-permute-start(bf16[64,1024]{1,0:T(8,128)(2,1)S(1)} %get-tuple-element.41.refs_0_), channel_id=1, source_target_pairs={{0,2},{2,0},{1,3},{3,1},{4,6},{6,4},{5,7},{7,5},{8,10},{10,8},{9,1... | collective-permute-start | bytes 393224 | tf_op jit(solution)/shard_map/ppermute | solution.py:260
  25.7 0.6 %adjoint_rest.1 = (bf16[64,1024]{1,0:T(8,128)(2,1)S(1)}, bf16[64,1024]{1,0:T(8,128)(2,1)S(1)}) custom-call(f32[64,2048]{1,0:T(8,128)S(1)} %get-tuple-element.37.adjoint, f32[16,16]{1,0:T(8,128)S(4)} %get-tuple-element.26.refs_3_.row_factor, bf16[256,256]{1,0:T(8,128)(2,1)S(1)} %get-tuple-element.35.wide_b, bf16[2,128,128]{2,1,0:T(8,128)(2,1)S(1)} %get-tuple-element.38.unmix_b), custom_call_target="tpu_custom_call" | custom-call | tf_op jit(solution)/shard_map/adjoint_rest/pallas_call | solution.py:407
  26.3 1.8 %collective-permute-start.5 = (bf16[64,1024]{1,0:T(8,128)(2,1)S(1)}, bf16[64,1024]{1,0:T(8,128)(2,1)S(1)}, u32[]{:S(2)}, u32[]{:S(2)}) collective-permute-start(bf16[64,1024]{1,0:T(8,128)(2,1)S(1)} %get-tuple-element.40), channel_id=1, source_target_pairs={{0,2},{2,0},{1,3},{3,1},{4,6},{6,4},{5,7},{7,5},{8,10},{10,8},{9,1... | collective-permute-start | bytes 393224 | tf_op jit(solution)/shard_map/ppermute | solution.py:260
  28.2 0.2 own.1.refs_0_
  28.4 2.0 %collective-permute-done.6.refs_1_ = bf16[64,1024]{1,0:T(8,128)(2,1)S(1)} collective-permute-done((bf16[64,1024]{1,0:T(8,128)(2,1)S(1)}, bf16[64,1024]{1,0:T(8,128)(2,1)S(1)}, u32[]{:S(2)}, u32[]{:S(2)}) %collective-permute-start.6) | collective-permute-done | bytes 131104 | tf_op jit(solution)/shard_map/ppermute | solution.py:260
  30.4 0.9 %finish_low.1.refs_2_ = bf16[32,2,2048]{2,1,0:T(2,128)(2,1)} custom-call(bf16[64,1024]{1,0:T(8,128)(2,1)S(1)} %get-tuple-element.41.refs_0_, bf16[64,1024]{1,0:T(8,128)(2,1)S(1)} %collective-permute-done.6.refs_1_, bf16[32,2,2048]{2,1,0:T(2,128)(2,1)S(1)} %get-tuple-element.24.refs_0_.probes.refs_2_, bf16[128,128]{1,0:T(8,128)(2,1)S(1)} %get-tuple-element.42.refs_3_), custom_call_target="tpu_custom_call" | custom-call | tf_op jit(solution)/shard_map/finish_low/pallas_call | solution.py:427
  31.3 0.5 %collective-permute-done.5.refs_1_ = bf16[64,1024]{1,0:T(8,128)(2,1)S(1)} collective-permute-done((bf16[64,1024]{1,0:T(8,128)(2,1)S(1)}, bf16[64,1024]{1,0:T(8,128)(2,1)S(1)}, u32[]{:S(2)}, u32[]{:S(2)}) %collective-permute-start.5) | collective-permute-done | bytes 131104 | tf_op jit(solution)/shard_map/ppermute | solution.py:260
  31.8 0.7 %finish_high.1 = bf16[32,2,2048]{2,1,0:T(2,128)(2,1)} custom-call(f32[64,1024]{1,0:T(8,128)S(1)} %own.1.refs_0_, bf16[64,1024]{1,0:T(8,128)(2,1)S(1)} %collective-permute-done.5.refs_1_, bf16[32,2,2048]{2,1,0:T(2,128)(2,1)} %finish_low.1.refs_2_), custom_call_target="tpu_custom_call", output_to_operand_aliasing={{}: (2, {})} | custom-call | tf_op jit(solution)/shard_map/finish_high/pallas_call | solution.py:436
  (1 shorter events, 0.0 us)
Async XLA Ops:
  0.0 9.5 %collective-permute-start = (bf16[32,2,2048]{2,1,0:T(2,128)(2,1)}, bf16[32,2,2048]{2,1,0:T(2,128)(2,1)S(1)}, u32[]{:S(2)}, u32[]{:S(2)}) collective-permute-start(bf16[32,2,2048]{2,1,0:T(2,128)(2,1)} %probes.1), channel_id=1, source_target_pairs={{0,2},{2,0},{1,3},{3,1},{4,6},{6,4},{5,7},{7,5},{8,10},{10,8},{9,1... | collective-permute-start | bytes 786440 | tf_op jit(solution)/shard_map/ppermute | solution.py:260
  11.1 5.6 %collective-permute-start.3 = (bf16[272,128]{1,0:T(8,128)(2,1)S(1)}, bf16[272,128]{1,0:T(8,128)(2,1)S(1)}, u32[]{:S(2)}, u32[]{:S(2)}) collective-permute-start(bf16[272,128]{1,0:T(8,128)(2,1)S(1)} %get-tuple-element.33), channel_id=1, source_target_pairs={{0,6},{2,4},{4,2},{6,0},{8,14},{10,12},{12,10},{14,8},{1,7},{3,5},... | collective-permute-start | bytes 208904 | tf_op jit(solution)/shard_map/ppermute | solution.py:273
  14.0 4.3 %collective-permute-start.2 = (bf16[272,128]{1,0:T(8,128)(2,1)S(1)}, bf16[272,128]{1,0:T(8,128)(2,1)S(1)}, u32[]{:S(2)}, u32[]{:S(2)}) collective-permute-start(bf16[272,128]{1,0:T(8,128)(2,1)S(1)} %get-tuple-element.33), channel_id=1, source_target_pairs={{0,4},{2,6},{4,0},{6,2},{8,12},{10,14},{12,8},{14,10},{1,5},{3,7},... | collective-permute-start | bytes 208904 | tf_op jit(solution)/shard_map/ppermute | solution.py:273
  14.4 4.3 %collective-permute-start.1 = (bf16[272,128]{1,0:T(8,128)(2,1)S(1)}, bf16[272,128]{1,0:T(8,128)(2,1)S(1)}, u32[]{:S(2)}, u32[]{:S(2)}) collective-permute-start(bf16[272,128]{1,0:T(8,128)(2,1)S(1)} %get-tuple-element.33), channel_id=1, source_target_pairs={{0,2},{2,0},{4,6},{6,4},{8,10},{10,8},{12,14},{14,12},{1,3},{3,1},... | collective-permute-start | bytes 208904 | tf_op jit(solution)/shard_map/ppermute | solution.py:273
  18.8 5.3 %collective-permute-start.4 = (bf16[272,128]{1,0:T(8,128)(2,1)S(1)}, bf16[272,128]{1,0:T(8,128)(2,1)S(1)}, u32[]{:S(2)}, u32[]{:S(2)}) collective-permute-start(bf16[272,128]{1,0:T(8,128)(2,1)S(1)} %get-tuple-element.43), channel_id=1, source_target_pairs={{0,8},{2,10},{4,12},{6,14},{8,0},{10,2},{12,4},{14,6},{1,9},{3,11}... | collective-permute-start | bytes 208904 | tf_op jit(solution)/shard_map/ppermute | solution.py:273
  25.4 5.0 %collective-permute-start.6 = (bf16[64,1024]{1,0:T(8,128)(2,1)S(1)}, bf16[64,1024]{1,0:T(8,128)(2,1)S(1)}, u32[]{:S(2)}, u32[]{:S(2)}) collective-permute-start(bf16[64,1024]{1,0:T(8,128)(2,1)S(1)} %get-tuple-element.41.refs_0_), channel_id=1, source_target_pairs={{0,2},{2,0},{1,3},{3,1},{4,6},{6,4},{5,7},{7,5},{8,10},{10,8},{9,1... | collective-permute-start | bytes 393224 | tf_op jit(solution)/shard_map/ppermute | solution.py:260
  26.3 5.5 %collective-permute-start.5 = (bf16[64,1024]{1,0:T(8,128)(2,1)S(1)}, bf16[64,1024]{1,0:T(8,128)(2,1)S(1)}, u32[]{:S(2)}, u32[]{:S(2)}) collective-permute-start(bf16[64,1024]{1,0:T(8,128)(2,1)S(1)} %get-tuple-element.40), channel_id=1, source_target_pairs={{0,2},{2,0},{1,3},{3,1},{4,6},{6,4},{5,7},{7,5},{8,10},{10,8},{9,1... | collective-permute-start | bytes 393224 | tf_op jit(solution)/shard_map/ppermute | solution.py:260
